TPU v7x, 32 devices: a whole 2x2x4 slice. The times are simulated.
32 devices in a mesh: replica: 4 (over y, core), shard: 8 (over z, x).
Axes of the slice: x: 2, y: 2, z: 4, core: 2. Of those that a mesh axis runs over, the one named last changes fastest.
Arguments:
- tokens: bfloat16 [32768, 768], P(('replica', 'shard')), may hold values from -6 to 6
- segment: int32 [32768], P(('replica', 'shard')), may hold values from 0 to 11, as said below
- norm_gain: bfloat16 [768], P('shard'), may hold values from 0.099609375 to 1.8984375
- w_in: bfloat16 [768, 3352], P('shard'), may hold values from -0.21875 to 0.21875
- conv_w: bfloat16 [4, 1792], P(None, 'shard'), may hold values from -3 to 3
- conv_b: bfloat16 [1792], P('shard'), may hold values from -3 to 3
- dt_bias: float32 [24], replicated, may hold values from -6 to -3
- a_log: float32 [24], replicated, may hold values from -6 to 1.4
- d_skip: float32 [24], replicated, may hold values from 0.5 to 1.5
- gate_gain: bfloat16 [1536], P('shard'), may hold values from 0.099609375 to 1.8984375
- w_out: bfloat16 [1536, 768], P('shard'), may hold values from -0.15625 to 0.15625
- cotangent: bfloat16 [32768, 768], P(('replica', 'shard')), may hold values from -6 to 6
Outputs:
- block_out: bfloat16 [32768, 768], P(('replica', 'shard'))
- grad_tokens: float32 [32768, 768], P(('replica', 'shard'))
- grad_norm_gain: float32 [768], P('shard')
- grad_w_in: float32 [768, 3352], P('shard')
- grad_conv_w: float32 [4, 1792], P(None, 'shard')
- grad_conv_b: float32 [1792], P('shard')
- grad_dt_bias: float32 [24], replicated
- grad_a_log: float32 [24], replicated
- grad_d_skip: float32 [24], replicated
- grad_gate_gain: float32 [1536], P('shard')
- grad_w_out: float32 [1536, 768], P('shard')
Inputs may be any that keep to these rules, and one draw needn't show every extreme that they name: `segment`: segment numbers start at 0 and rise by one at each new document, never falling, across all 32768 tokens. Each replica group's 8192 tokens begin a new document and are exactly 3 documents of 1024 to 4096 tokens packed back to back; each group holds one of exactly 4096 tokens.
All inputs are finite; a program needn't handle non-finite values.
Results may differ from a plain program's by a relative error of at most 0.019.
Values may be sent and summed in bfloat16 or wider, within the bound.
A program may use at most 192 MiB of HBM per device.

v0:
```python
import jax
import jax.numpy as jnp
from jax import lax
from jax.sharding import PartitionSpec as P

H = 24
P_SIZE = 64
N = 128
KC = 4
SPAN = 256
DI = 1536
CONV = 1792


EPSILON = 1e-05
WRAP_IDS = 256


def passed_along(shard, axis, by):
    count = lax.axis_size(axis)
    pairs = [(i, i + by) for i in range(count) if 0 <= i + by < count]
    return lax.ppermute(shard, axis, pairs)


def prefix(shard, axis, combine, identity, reverse):
    count, mine = (lax.axis_size(axis), lax.axis_index(axis))
    everything = jax.tree.map(
        lambda part, kind: lax.all_gather(part.astype(kind), axis),
        shard,
        (jnp.bfloat16, jnp.bfloat16),
    )
    start = jax.tree.map(
        lambda part, zero: jnp.broadcast_to(jnp.asarray(zero, part.dtype), part.shape),
        shard,
        identity,
    )

    def lap(k, before):
        at = count - 1 - k if reverse else k
        reached = at > mine if reverse else at < mine
        new = combine(
            before, jax.tree.map(lambda part, own: part[at].astype(own.dtype), everything, shard)
        )
        return jax.tree.map(lambda a, b: jnp.where(reached, a, b), new, before)

    return lax.fori_loop(0, count, lap, start)


def rms_scale(values, gain_vec):
    return (
        values * lax.rsqrt(jnp.mean(values * values, axis=-1, keepdims=True) + EPSILON) * gain_vec
    )


def causal_conv(xbc_in, rim_in, weight_in, bias_in, segment_ids, rim_segments):
    width = weight_in.shape[0]
    length = xbc_in.shape[0]
    row_block = jnp.concatenate([rim_in, xbc_in], axis=0)
    seg_block = jnp.concatenate([rim_segments, segment_ids], axis=0)
    summed = jnp.zeros_like(xbc_in) + bias_in[None, :]
    for offset in range(width):
        kept_mask = (seg_block[offset : offset + length] == segment_ids).astype(jnp.float32)
        summed = (
            summed
            + weight_in[offset][None, :] * row_block[offset : offset + length] * kept_mask[:, None]
        )
    return jax.nn.silu(summed)


def log_decay(raw_in, bias_in, alog_in):
    step_size = jax.nn.softplus(raw_in + bias_in[None, :])
    return (step_size, -jnp.exp(alog_in)[None, :] * step_size)


def gated_norm(mixed_in, gate_in, gain_in):
    product = mixed_in * jax.nn.silu(gate_in)
    return (
        product
        * lax.rsqrt(jnp.mean(product * product, axis=-1, keepdims=True) + EPSILON)
        * gain_in[None, :]
    )


def state_space(
    flat_input,
    b_mat,
    c_mat,
    step_size,
    decay_rate,
    segment_ids,
    state_init,
    prev_segment,
    block_len,
):
    length, inner = flat_input.shape
    head_count = step_size.shape[1]
    head_dim = inner // head_count
    block_count = length // block_len
    inputs = (
        flat_input.reshape(block_count, block_len, inner),
        b_mat.reshape(block_count, block_len, -1),
        c_mat.reshape(block_count, block_len, -1),
        step_size.reshape(block_count, block_len, head_count).transpose(0, 2, 1),
        decay_rate.reshape(block_count, block_len, head_count).transpose(0, 2, 1),
        segment_ids.reshape(block_count, block_len),
    )
    causal_mask = jnp.tril(jnp.ones((block_len, block_len), dtype=bool))

    def one_block(carry, block):
        state, last_segment = carry
        x_block, b_block, c_block, dt_block, a_block, s_block = block
        cumulative = jnp.cumsum(a_block, axis=1)
        same_doc = (s_block[:, None] == s_block[None, :]) & causal_mask
        decays = jnp.exp(
            jnp.where(
                same_doc[None, :, :], cumulative[:, :, None] - cumulative[:, None, :], -jnp.inf
            )
        )
        scores = jnp.dot(c_block, b_block.T, preferred_element_type=jnp.float32)
        scaled_x = x_block.reshape(block_len, head_count, head_dim) * dt_block.T[:, :, None]
        within = jnp.einsum(
            "hts,shp->thp",
            decays * scores[None, :, :],
            scaled_x,
            preferred_element_type=jnp.float32,
        )
        entering = jnp.exp(cumulative) * (s_block == last_segment).astype(jnp.float32)[None, :]
        from_state = (
            jnp.einsum("tn,hpn->thp", c_block, state, preferred_element_type=jnp.float32)
            * entering.T[:, :, None]
        )
        leaving = (
            jnp.exp(cumulative[:, -1:] - cumulative)
            * (s_block == s_block[-1]).astype(jnp.float32)[None, :]
        )
        passing = jnp.exp(cumulative[:, -1]) * (s_block[-1] == last_segment).astype(jnp.float32)
        new_state = state * passing[:, None, None] + jnp.einsum(
            "hs,sn,shp->hpn", leaving, b_block, scaled_x, preferred_element_type=jnp.float32
        )
        return ((new_state, s_block[-1]), (within + from_state).reshape(block_len, inner))

    (final_state, last_seen), outputs = lax.scan(
        jax.checkpoint(one_block), (state_init, prev_segment), inputs
    )
    return (outputs.reshape(length, inner), final_state)


def carry_combine(earlier, later):
    gain_early, state_early = earlier
    gain_late, state_late = later
    return (gain_early * gain_late, state_early * gain_late[:, None, None] + state_late)


def body(
    tokens,
    segment,
    norm_gain,
    w_in,
    conv_w,
    conv_b,
    dt_bias,
    a_log,
    d_skip,
    gate_gain,
    w_out,
    cotangent,
):
    gathered = (
        lax.all_gather(w_in, "shard", axis=0, tiled=True),
        lax.all_gather(w_out, "shard", axis=0, tiled=True),
        lax.all_gather(conv_w, "shard", axis=1, tiled=True),
        lax.all_gather(conv_b, "shard", axis=0, tiled=True),
        lax.all_gather(norm_gain, "shard", axis=0, tiled=True),
        lax.all_gather(gate_gain, "shard", axis=0, tiled=True),
    )
    full_in, full_out, full_conv, full_bias, full_norm, full_gate = gathered
    rim_len = KC - 1
    wrapped = segment % WRAP_IDS
    tok_f = tokens.astype(jnp.float32)
    normed_b = rms_scale(tok_f, full_norm.astype(jnp.float32)[None, :]).astype(jnp.bfloat16)
    projected = jnp.dot(normed_b, full_in, preferred_element_type=jnp.float32).astype(jnp.bfloat16)
    xbc_b = projected[:, DI : DI + CONV]
    rim_rows, rim_segs = passed_along(
        (xbc_b[-rim_len:], wrapped[-rim_len:].astype(jnp.bfloat16)), "shard", 1
    )
    prev_segs = rim_segs.astype(jnp.int32)
    prev_last = prev_segs[-1]
    xbc_f = xbc_b.astype(jnp.float32)
    rim_f = rim_rows.astype(jnp.float32)
    gate_z = projected[:, :DI].astype(jnp.float32)
    dt_raw = projected[:, DI + CONV :].astype(jnp.float32)
    tok_count = tokens.shape[0]

    def conv_piece(xbc_in, rim_in, weight_in, bias_in):
        return causal_conv(xbc_in, rim_in, weight_in, bias_in, wrapped, prev_segs)

    def ssd_piece(conv_in, raw_in, bias_in, alog_in, skip_in, state_in):
        flat_input = conv_in[:, :DI]
        b_mat = conv_in[:, DI : DI + N]
        c_part = conv_in[:, DI + N :]
        step_size, decay_rate = log_decay(raw_in, bias_in, alog_in)
        mixed_part, final_state = state_space(
            flat_input, b_mat, c_part, step_size, decay_rate, wrapped, state_in, prev_last, SPAN
        )
        return (mixed_part + jnp.repeat(skip_in, P_SIZE)[None, :] * flat_input, final_state)

    def gate_piece(mixed_in, gate_in, gain_in):
        return gated_norm(mixed_in, gate_in, gain_in)

    conv_out = conv_piece(
        xbc_f, rim_f, full_conv.astype(jnp.float32), full_bias.astype(jnp.float32)
    )
    conv_f = lax.optimization_barrier(conv_out.astype(jnp.bfloat16)).astype(jnp.float32)
    zero_state = jnp.zeros((H, P_SIZE, N), jnp.float32)
    local_mixed, local_state = ssd_piece(conv_f, dt_raw, dt_bias, a_log, d_skip, zero_state)
    unused_step, decay_rate = log_decay(dt_raw, dt_bias, a_log)
    running = (
        jnp.exp(jnp.cumsum(decay_rate, axis=0))
        * (wrapped == prev_last).astype(jnp.float32)[:, None]
    )
    carry_gain = running[-1]
    identity = (jnp.ones((H,), jnp.float32), zero_state)
    unused_gain, state_in = prefix(
        (carry_gain, local_state), "shard", carry_combine, identity, False
    )
    c_mat = conv_f[:, DI + N :]
    from_carry = (
        jnp.einsum("tn,hpn->thp", c_mat, state_in, preferred_element_type=jnp.float32)
        * running[:, :, None]
    )
    mixed_out = local_mixed + from_carry.reshape(tok_count, DI)
    gated_out = gate_piece(mixed_out, gate_z, full_gate.astype(jnp.float32))
    gated_b = gated_out.astype(jnp.bfloat16)
    branch = jnp.dot(gated_b, full_out, preferred_element_type=jnp.float32)
    block_out = (tok_f + branch).astype(jnp.bfloat16)
    regathered = (
        lax.all_gather(w_in, "shard", axis=0, tiled=True),
        lax.all_gather(w_out, "shard", axis=0, tiled=True),
        lax.all_gather(conv_w, "shard", axis=1, tiled=True),
        lax.all_gather(conv_b, "shard", axis=0, tiled=True),
        lax.all_gather(norm_gain, "shard", axis=0, tiled=True),
        lax.all_gather(gate_gain, "shard", axis=0, tiled=True),
    )
    back_in, back_out, back_conv, back_bias, back_norm, back_gate = regathered
    g_gated = lax.dot_general(
        cotangent, back_out, (((1,), (1,)), ((), ())), preferred_element_type=jnp.float32
    )
    grad_out_full = lax.dot_general(
        gated_b, cotangent, (((0,), (0,)), ((), ())), preferred_element_type=jnp.float32
    )
    unused_gated, gate_pull = jax.vjp(gate_piece, mixed_out, gate_z, back_gate.astype(jnp.float32))
    g_mixed, g_gate_z, g_gate_gain = gate_pull(g_gated)
    g_heads = g_mixed.reshape(tok_count, H, P_SIZE)
    seed_grad = jnp.einsum(
        "thp,tn,th->hpn", g_heads, c_mat, running, preferred_element_type=jnp.float32
    )
    unused_back, state_out_grad = prefix(
        (carry_gain, seed_grad), "shard", carry_combine, identity, True
    )
    unused_pair, ssd_pull = jax.vjp(ssd_piece, conv_f, dt_raw, dt_bias, a_log, d_skip, state_in)
    g_conv, g_dt_raw, g_dt_bias, g_a_log, g_d_skip, unused_state = ssd_pull(
        (g_mixed, state_out_grad)
    )
    unused_conv, conv_pull = jax.vjp(
        conv_piece, xbc_f, rim_f, back_conv.astype(jnp.float32), back_bias.astype(jnp.float32)
    )
    g_xbc, g_rim, g_conv_w, g_conv_b = conv_pull(g_conv)
    from_next = passed_along(g_rim, "shard", -1)
    g_xbc = g_xbc + jnp.pad(from_next, ((g_xbc.shape[0] - rim_len, 0), (0, 0)))
    g_projected = jnp.concatenate([g_gate_z, g_xbc, g_dt_raw], axis=1).astype(jnp.bfloat16)
    grad_in_full = lax.dot_general(
        normed_b, g_projected, (((0,), (0,)), ((), ())), preferred_element_type=jnp.float32
    )
    g_normed = lax.dot_general(
        g_projected, back_in, (((1,), (1,)), ((), ())), preferred_element_type=jnp.float32
    )

    def norm_piece(tok_in, gain_in):
        return rms_scale(tok_in, gain_in[None, :])

    unused_norm, norm_pull = jax.vjp(norm_piece, tok_f, back_norm.astype(jnp.float32))
    g_tokens, g_norm_gain = norm_pull(g_normed)
    grad_tokens = cotangent.astype(jnp.float32) + g_tokens
    shares = (
        lax.psum_scatter(grad_in_full, "shard", scatter_dimension=0, tiled=True),
        lax.psum_scatter(grad_out_full, "shard", scatter_dimension=0, tiled=True),
        lax.psum_scatter(g_conv_w, "shard", scatter_dimension=1, tiled=True),
        lax.psum_scatter(g_conv_b, "shard", scatter_dimension=0, tiled=True),
        lax.psum_scatter(g_norm_gain, "shard", scatter_dimension=0, tiled=True),
        lax.psum_scatter(g_gate_gain, "shard", scatter_dimension=0, tiled=True),
    )
    part_in, part_out, part_conv, part_bias, part_norm, part_gate = shares
    summed = lax.psum((part_in, part_out, part_conv, part_bias, part_norm, part_gate), "replica")
    head_sums = lax.psum((g_dt_bias, g_a_log, g_d_skip), ("replica", "shard"))
    return (
        block_out,
        grad_tokens,
        summed[4],
        summed[0],
        summed[2],
        summed[3],
        head_sums[0],
        head_sums[1],
        head_sums[2],
        summed[5],
        summed[1],
    )


def solution(mesh):
    in_specs = (
        P(("replica", "shard"), None),
        P(("replica", "shard")),
        P("shard"),
        P("shard", None),
        P(None, "shard"),
        P("shard"),
        P(),
        P(),
        P(),
        P("shard"),
        P("shard", None),
        P(("replica", "shard"), None),
    )
    out_specs = (
        P(("replica", "shard"), None),
        P(("replica", "shard"), None),
        P("shard"),
        P("shard", None),
        P(None, "shard"),
        P("shard"),
        P(),
        P(),
        P(),
        P("shard"),
        P("shard", None),
    )
    return jax.shard_map(body, mesh=mesh, in_specs=in_specs, out_specs=out_specs, check_vma=False)
```

profile of v0, /device:TPU:0, one launch (start us, length us, event | category | flops | bytes accessed | tf_op | source)
XLA Modules:
  0.0 1299.4 jit_solution(10414025319103159735)
XLA Ops:
  19.4 36.3 %all-reduce.24 = (bf16[768]{0:T(1024)(128)(2,1)S(1)}, bf16[1792]{0:T(1024)(128)(2,1)S(1)}, bf16[1536]{0:T(1024)(128)(2,1)S(1)}) all-reduce(bf16[768]{0:T(1024)(128)(2,1)S(1)} %dynamic-update-slice, bf16[1792]{0:T(1024)(128)(2,1)S(1)} %dynamic-update-slice.1, ...), channel_id=1, replica_groups=mesh['replica'=4,'shard'=8] {'shard'}, use_global_device_ids=true, to_apply=%add.14 | all-reduce | flops 4096 | bytes 16384
  55.8 26.7 %all-gather.2 = bf16[8,224,4]{1,2,0:T(4,128)(2,1)S(1)} all-gather(bf16[1,224,4]{1,2,0:T(4,128)(2,1)} %bitcast.477), channel_id=1, replica_groups=mesh['replica'=4,'shard'=8] {'shard'}, dimensions={0}, use_global_device_ids=true | all-gather | bytes 16128 | tf_op jit(solution)/shard_map/all_gather | solution.py:171
  146.7 215.4 %while.88 = (s32[]{:T(128)}, f32[24,64,128]{2,1,0:T(8,128)}, s32[]{:T(128)}, f32[4,256,1536]{1,0,2:T(4,128)}, f32[4,24,256]{2,1,0:T(8,128)}, /*index=5*/s32[4,25...) while((s32[]{:T(128)}, f32[24,64,128]{2,1,0:T(8,128)}, ...), condition=%wide.region_4.5_spmd.clone, body=%wide.region_1.4_spmd.clone.sunk | while | flops 427910240 | bytes 21082408 | solution.py:142
  162.7 34.2 %dynamic_update_slice.85 = f32[4,256,1536]{1,0,2:T(4,128)} dynamic-update-slice(f32[4,256,1536]{1,0,2:T(4,128)} %get-tuple-element.1620, f32[1,256,1536]{1,0,2:T(1,128)S(1)} %copy.404, s32[]{:T(128)} %get-tuple-element.1617, s32[]{:T(128)} %constant.228.clone.1..sunk.2, s32[]{:T(128)} %constant.228.clone.1..sunk.2) | dynamic-update-slice | bytes 3145732 | tf_op jit(solution)/shard_map/while/body/jit(dynamic_update_index_in_dim)/dynamic_update_slice | solution.py:142
  215.8 34.2 %dynamic_update_slice.85 = f32[4,256,1536]{1,0,2:T(4,128)} dynamic-update-slice(f32[4,256,1536]{1,0,2:T(4,128)} %get-tuple-element.1620, f32[1,256,1536]{1,0,2:T(1,128)S(1)} %copy.404, s32[]{:T(128)} %get-tuple-element.1617, s32[]{:T(128)} %constant.228.clone.1..sunk.2, s32[]{:T(128)} %constant.228.clone.1..sunk.2) | dynamic-update-slice | bytes 3145732 | tf_op jit(solution)/shard_map/while/body/jit(dynamic_update_index_in_dim)/dynamic_update_slice | solution.py:142
  270.0 34.2 %dynamic_update_slice.85 = f32[4,256,1536]{1,0,2:T(4,128)} dynamic-update-slice(f32[4,256,1536]{1,0,2:T(4,128)} %get-tuple-element.1620, f32[1,256,1536]{1,0,2:T(1,128)S(1)} %copy.404, s32[]{:T(128)} %get-tuple-element.1617, s32[]{:T(128)} %constant.228.clone.1..sunk.2, s32[]{:T(128)} %constant.228.clone.1..sunk.2) | dynamic-update-slice | bytes 3145732 | tf_op jit(solution)/shard_map/while/body/jit(dynamic_update_index_in_dim)/dynamic_update_slice | solution.py:142
  324.2 34.2 %dynamic_update_slice.85 = f32[4,256,1536]{1,0,2:T(4,128)} dynamic-update-slice(f32[4,256,1536]{1,0,2:T(4,128)} %get-tuple-element.1620, f32[1,256,1536]{1,0,2:T(1,128)S(1)} %copy.404, s32[]{:T(128)} %get-tuple-element.1617, s32[]{:T(128)} %constant.228.clone.1..sunk.2, s32[]{:T(128)} %constant.228.clone.1..sunk.2) | dynamic-update-slice | bytes 3145732 | tf_op jit(solution)/shard_map/while/body/jit(dynamic_update_index_in_dim)/dynamic_update_slice | solution.py:142
  374.7 20.6 %all-gather.3 = bf16[8,1,24]{2,1,0:T(2,128)(2,1)S(1)} all-gather(bf16[1,1,24]{2,1,0:T(2,128)(2,1)S(1)} %bitcast.479), channel_id=1, replica_groups=mesh['replica'=4,'shard'=8] {'shard'}, dimensions={0}, use_global_device_ids=true | all-gather | bytes 432 | tf_op jit(solution)/shard_map/all_gather | solution.py:28
  408.4 18.3 %all-gather.13.cloned.1.call-done = bf16[192,64,128]{2,1,0:T(8,128)(2,1)} async-done(((bf16[24,64,128]{2,1,0:T(8,128)(2,1)}), bf16[192,64,128]{2,1,0:T(8,128)(2,1)}) %all-gather.13.cloned.1.call-update) | async-done | bytes 3145744 | tf_op jit(solution)/shard_map/all_gather | solution.py:28
  456.6 23.1 %all-gather.11.cloned.1.call-done = bf16[1536,768]{1,0:T(8,128)(2,1)} async-done(((bf16[192,768]{1,0:T(8,128)(2,1)}), bf16[1536,768]{1,0:T(8,128)(2,1)}) %all-gather.11.cloned.1.call-update) | async-done | bytes 2359312 | tf_op jit(solution)/shard_map/all_gather | solution.py:170
  487.3 14.4 %multiply_reduce_fusion.10 = (f32[1536]{0:T(1024)}, f32[1024,1536]{0,1:T(8,128)}, bf16[1024,1536]{0,1:T(8,128)(2,1)}) fusion(f32[1024,1792]{0,1:T(8,128)} %convert_element_type.190, bf16[1024,3352]{0,1:T(8,128)(2,1)} %copy-done.7, f32[1024,1536]{0,1:T(8,128)} %get-tuple-element.1204, f32[1024]{0:T(1024)S(1)} %multiply_multiply_fusion.5, ...), kind=kLoop, calls=%fused_computation.202 | loop fusion | flops 33028608 | bytes 37769216 | tf_op jit(solution)/shard_map/transpose(jvp())/reduce_sum | solution.py:205
  514.4 33.5 %while.86 = (s32[]{:T(128)}, f32[24,64,128]{2,1,0:T(8,128)S(1)}, s32[]{:T(128)}, f32[4,24,64,128]{3,2,1,0:T(8,128)}, s32[4]{0:T(128)S(1)}, /*index=5*/f32[4,24,2...) while((s32[]{:T(128)}, f32[24,64,128]{2,1,0:T(8,128)S(1)}, ...), condition=%wide.region_16.17_spmd, body=%wide.region_13.16_spmd.sunk | while | flops 102648416 | bytes 8329507 | solution.py:142
  548.0 25.5 %all-gather.15.cloned.1.call-done = bf16[192,64,128]{2,1,0:T(8,128)(2,1)} async-done(((bf16[24,64,128]{2,1,0:T(8,128)(2,1)}), bf16[192,64,128]{2,1,0:T(8,128)(2,1)}) %all-gather.15.cloned.1.call-update) | async-done | bytes 3145744 | tf_op jit(solution)/shard_map/all_gather | solution.py:28
  589.9 311.4 %while.87 = (s32[]{:T(128)}, f32[24,64,128]{2,1,0:T(8,128)S(1)}, f32[4,256,1536]{1,0,2:T(4,128)}, f32[4,256,128]{2,1,0:T(8,128)}, f32[4,256,128]{2,1,0:T(8,128)}...) while((s32[]{:T(128)}, f32[24,64,128]{2,1,0:T(8,128)S(1)}, ...), condition=%wide.region_29.30_spmd.clone, body=%wide.region_17.29_spmd.clone.sunk | while | flops 983723200 | bytes 62036488 | solution.py:142
  629.0 34.4 %dynamic_update_slice.84 = f32[4,256,1536]{1,0,2:T(4,128)} dynamic-update-slice(f32[4,256,1536]{1,0,2:T(4,128)} %get-tuple-element.1757, f32[1,256,1536]{1,0,2:T(1,128)} %copy.398, s32[]{:T(128)S(6)} %sub.245, s32[]{:T(128)} %constant.228.clone.1..sunk.1, s32[]{:T(128)} %constant.228.clone.1..sunk.1) | dynamic-update-slice | bytes 3145732 | tf_op jit(solution)/shard_map/transpose(jvp())/while/body/jit(dynamic_update_index_in_dim)/dynamic_update_slice | solution.py:142
  706.9 34.3 %dynamic_update_slice.84 = f32[4,256,1536]{1,0,2:T(4,128)} dynamic-update-slice(f32[4,256,1536]{1,0,2:T(4,128)} %get-tuple-element.1757, f32[1,256,1536]{1,0,2:T(1,128)} %copy.398, s32[]{:T(128)S(6)} %sub.245, s32[]{:T(128)} %constant.228.clone.1..sunk.1, s32[]{:T(128)} %constant.228.clone.1..sunk.1) | dynamic-update-slice | bytes 3145732 | tf_op jit(solution)/shard_map/transpose(jvp())/while/body/jit(dynamic_update_index_in_dim)/dynamic_update_slice | solution.py:142
  784.6 34.3 %dynamic_update_slice.84 = f32[4,256,1536]{1,0,2:T(4,128)} dynamic-update-slice(f32[4,256,1536]{1,0,2:T(4,128)} %get-tuple-element.1757, f32[1,256,1536]{1,0,2:T(1,128)} %copy.398, s32[]{:T(128)S(6)} %sub.245, s32[]{:T(128)} %constant.228.clone.1..sunk.1, s32[]{:T(128)} %constant.228.clone.1..sunk.1) | dynamic-update-slice | bytes 3145732 | tf_op jit(solution)/shard_map/transpose(jvp())/while/body/jit(dynamic_update_index_in_dim)/dynamic_update_slice | solution.py:142
  862.4 34.3 %dynamic_update_slice.84 = f32[4,256,1536]{1,0,2:T(4,128)} dynamic-update-slice(f32[4,256,1536]{1,0,2:T(4,128)} %get-tuple-element.1757, f32[1,256,1536]{1,0,2:T(1,128)} %copy.398, s32[]{:T(128)S(6)} %sub.245, s32[]{:T(128)} %constant.228.clone.1..sunk.1, s32[]{:T(128)} %constant.228.clone.1..sunk.1) | dynamic-update-slice | bytes 3145732 | tf_op jit(solution)/shard_map/transpose(jvp())/while/body/jit(dynamic_update_index_in_dim)/dynamic_update_slice | solution.py:142
  952.2 14.6 %pad_add_fusion = f32[1027,1792]{0,1:T(8,128)} fusion(f32[1024,1792]{0,1:T(8,128)} %copy-done.3, f32[1024,1792]{0,1:T(8,128)} %get-tuple-element.1230, f32[1024,1792]{0,1:T(8,128)} %get-tuple-element.1231, f32[1024,1792]{0,1:T(8,128)} %copy-done.2), kind=kLoop, calls=%fused_computation.171 | loop fusion | flops 5521152 | bytes 36721664 | tf_op jit(solution)/shard_map/transpose(jvp())/add_any | solution.py:65
  1000.7 44.8 %all-reduce.20 = (f32[24]{0:T(128)}, f32[24]{0:T(128)}, f32[24]{0:T(128)}) all-reduce(f32[24]{0:T(128)S(1)} %get-tuple-element.1200, f32[24]{0:T(128)S(1)} %negate_multiply_fusion, f32[24]{0:T(128)S(1)} %reduce_sum.301), channel_id=1, replica_groups=mesh['replica'=4,'shard'=8] {'replica','shard'}, use_global_device_ids=true, to_apply=%region_46.47 | all-reduce | flops 72 | bytes 576 | tf_op jit(solution)/shard_map/psum | solution.py:294
  1045.5 125.9 %reduce-scatter.6.cloned.1.call-done = f32[96,3352]{1,0:T(8,128)} async-done(((f32[768,3352]{1,0:T(8,128)}), f32[96,3352]{1,0:T(8,128)}) %reduce-scatter.6.cloned.1.call-update) | async-done | bytes 1287184 | tf_op jit(solution)/shard_map/reduce_scatter | solution.py:285
  1182.8 35.2 %all-reduce.21 = (f32[768]{0:T(1024)S(1)}, f32[1792]{0:T(1024)S(1)}, f32[1536]{0:T(1024)S(1)}) all-reduce(f32[768]{0:T(1024)S(1)} %get-tuple-element.1083, f32[1792]{0:T(1024)S(1)} %get-tuple-element.1081, f32[1536]{0:T(1024)S(1)} %copy-done.52), channel_id=4, replica_groups=mesh['replica'=4,'shard'=8] {'shard'}, use_global_device_ids=true, to_apply=%region_32.33.clone | all-reduce | flops 4096 | bytes 32768
  1222.7 15.0 %reduce-scatter.10.cloned.1.call-done = f32[224,4]{1,0:T(8,128)} async-done(((f32[1792,4]{1,0:T(8,128)}), f32[224,4]{1,0:T(8,128)}) %reduce-scatter.10.cloned.1.call-update) | async-done | bytes 3600
  1245.0 42.9 %all-reduce.27.cloned.1.call-done = (f32[96,3352]{1,0:T(8,128)}, f32[192,768]{1,0:T(8,128)}) async-done(((f32[96,3352]{1,0:T(8,128)}, f32[192,768]{1,0:T(8,128)}), (f32[96,3352]{1,0:T(8,128)}, f32[192,768]{1,0:T(8,128)})) %all-reduce.27.cloned.1.call-update) | async-done | bytes 1877008 | tf_op jit(solution)/shard_map/psum | solution.py:293
  (683 shorter events, 564.4 us)
Async XLA Ops:
  7.2 93.7 %all-gather.9.cloned.1.call-start = ((), (), s32[]{:S(2)}) async-start(), calls=%async_computation.3 | async-start | bytes 5971968 | tf_op jit(solution)/shard_map/all_gather | solution.py:169
  7.9 418.8 %all-gather.13.cloned.1.call-start = ((), (), s32[]{:S(2)}) async-start(), calls=%async_computation.7 | async-start | bytes 3538944 | tf_op jit(solution)/shard_map/all_gather | solution.py:28
  8.7 76.5 %collective-permute-start = (bf16[3]{0:T(256)(128)(2,1)S(1)}, bf16[3]{0:T(256)(128)(2,1)S(1)}, u32[]{:S(2)}, u32[]{:S(2)}) collective-permute-start(bf16[3]{0:T(256)(128)(2,1)S(1)} %slice.173), channel_id=1, source_target_pairs={{0,1},{1,2},{2,3},{3,4},{4,5},{5,6},{6,7},{8,9},{9,10},{10,11},{11... | collective-permute-start | bytes 26 | tf_op jit(solution)/shard_map/ppermute | solution.py:22
  55.8 54.1 %copy-start.45 = (f32[768]{0:T(1024)}, f32[768]{0:T(1024)S(1)}, u32[]{:S(2)}) copy-start(f32[768]{0:T(1024)S(1)} %convert_element_type.178) | copy-start | bytes 9220
  111.0 11.4 collective-permute-start.1
  146.7 219.0 %copy-start.51 = (s32[1024]{0:T(1024)S(1)}, s32[1024]{0:T(1024)}, u32[]{:S(2)}) copy-start(s32[1024]{0:T(1024)} %param.23) | copy-start | bytes 12292
  364.1 115.6 %all-gather.11.cloned.1.call-start = ((), (), s32[]{:S(2)}) async-start(), calls=%async_computation.4 | async-start | bytes 2654208 | tf_op jit(solution)/shard_map/all_gather | solution.py:170
  364.8 208.7 %all-gather.15.cloned.1.call-start = ((), (), s32[]{:S(2)}) async-start(), calls=%async_computation.8 | async-start | bytes 3538944 | tf_op jit(solution)/shard_map/all_gather | solution.py:28
  365.7 73.1 %copy-start.32 = (f32[1536]{0:T(1024)}, f32[1536]{0:T(1024)S(1)}, u32[]{:S(2)}) copy-start(f32[1536]{0:T(1024)S(1)} %mul.857) | copy-start | bytes 18436
  365.7 121.6 %copy-start.42 = (f32[1536]{0:T(1024)}, f32[1536]{0:T(1024)S(1)}, u32[]{:S(2)}) copy-start(f32[1536]{0:T(1024)S(1)} %convert_element_type.194) | copy-start | bytes 18436
  514.3 531.2 %reduce-scatter.8.cloned.1.call-start = ((), (), s32[]{:S(2)}) async-start(), calls=%async_computation.6 | async-start | bytes 5308416 | tf_op jit(solution)/shard_map/reduce_scatter | solution.py:286
  548.0 623.5 %reduce-scatter.6.cloned.1.call-start = ((), (), s32[]{:S(2)}) async-start(), calls=%async_computation.5 | async-start | bytes 11943936 | tf_op jit(solution)/shard_map/reduce_scatter | solution.py:285
  619.4 47.9 %copy-start.15 = (f32[256,24]{0,1:T(8,128)S(1)}, f32[256,24]{0,1:T(8,128)}, u32[]{:S(2)}) copy-start(f32[256,24]{0,1:T(8,128)} %copy-done.14) | copy-start | bytes 73732 | tf_op jit(solution)/shard_map/transpose(jvp())/while
  621.3 46.5 %copy-start.9 = (bf16[4,256,128]{2,1,0:T(8,128)(2,1)S(1)}, bf16[4,256,128]{2,1,0:T(8,128)(2,1)}, u32[]{:S(2)}) copy-start(bf16[4,256,128]{2,1,0:T(8,128)(2,1)} %copy-done.8) | copy-start | bytes 786436 | tf_op jit(solution)/shard_map/transpose(jvp())/while
  697.3 47.9 %copy-start.15 = (f32[256,24]{0,1:T(8,128)S(1)}, f32[256,24]{0,1:T(8,128)}, u32[]{:S(2)}) copy-start(f32[256,24]{0,1:T(8,128)} %copy-done.14) | copy-start | bytes 73732 | tf_op jit(solution)/shard_map/transpose(jvp())/while
  699.2 46.5 %copy-start.9 = (bf16[4,256,128]{2,1,0:T(8,128)(2,1)S(1)}, bf16[4,256,128]{2,1,0:T(8,128)(2,1)}, u32[]{:S(2)}) copy-start(bf16[4,256,128]{2,1,0:T(8,128)(2,1)} %copy-done.8) | copy-start | bytes 786436 | tf_op jit(solution)/shard_map/transpose(jvp())/while
  775.1 47.9 %copy-start.15 = (f32[256,24]{0,1:T(8,128)S(1)}, f32[256,24]{0,1:T(8,128)}, u32[]{:S(2)}) copy-start(f32[256,24]{0,1:T(8,128)} %copy-done.14) | copy-start | bytes 73732 | tf_op jit(solution)/shard_map/transpose(jvp())/while
  777.0 46.5 %copy-start.9 = (bf16[4,256,128]{2,1,0:T(8,128)(2,1)S(1)}, bf16[4,256,128]{2,1,0:T(8,128)(2,1)}, u32[]{:S(2)}) copy-start(bf16[4,256,128]{2,1,0:T(8,128)(2,1)} %copy-done.8) | copy-start | bytes 786436 | tf_op jit(solution)/shard_map/transpose(jvp())/while
  852.8 47.9 %copy-start.15 = (f32[256,24]{0,1:T(8,128)S(1)}, f32[256,24]{0,1:T(8,128)}, u32[]{:S(2)}) copy-start(f32[256,24]{0,1:T(8,128)} %copy-done.14) | copy-start | bytes 73732 | tf_op jit(solution)/shard_map/transpose(jvp())/while
  950.8 17.2 %collective-permute-start.2 = (f32[3,1792]{1,0:T(4,128)S(1)}, f32[3,1792]{1,0:T(4,128)S(1)}, u32[]{:S(2)}, u32[]{:S(2)}) collective-permute-start(f32[3,1792]{1,0:T(4,128)S(1)} %copy.271), channel_id=1, source_target_pairs={{1,0},{2,1},{3,2},{4,3},{5,4},{6,5},{7,6},{9,8},{10,9},{11,10},{12... | collective-permute-start | bytes 64520 | tf_op jit(solution)/shard_map/ppermute | solution.py:22
  989.3 248.4 %reduce-scatter.10.cloned.1.call-start = ((), (), s32[]{:S(2)}) async-start(), calls=%async_computation.9 | async-start | bytes 1032192
  1000.6 287.3 %all-reduce.27.cloned.1.call-start = ((), (), s32[]{:S(2)}) async-start(), calls=%async_computation.10 | async-start | bytes 3833856 | tf_op jit(solution)/shard_map/psum | solution.py:293
  1171.5 46.8 %copy-start.41 = (f32[1024]{0:T(1024)S(1)}, f32[1024]{0:T(1024)}, u32[]{:S(2)}) copy-start(f32[1024]{0:T(1024)} %copy-done.40) | copy-start | bytes 12292
  1171.5 46.8 %copy-start.23 = (bf16[1024,768]{1,0:T(8,128)(2,1)S(1)}, bf16[1024,768]{1,0:T(8,128)(2,1)}, u32[]{:S(2)}) copy-start(bf16[1024,768]{1,0:T(8,128)(2,1)} %param.33) | copy-start | bytes 4718596
  (75 other events, 1053.4 us)
Sparse Core Ops, SparseCore 0:
  10.2 90.6 all-gather.8
  364.2 62.4 all-gather.12
  428.9 50.6 all-gather.10
  514.4 59.0 all-gather.14
  577.0 93.9 reduce-scatter.7
  989.4 181.9 reduce-scatter.5
  1175.7 61.9 reduce-scatter.9
  1240.1 47.7 all-reduce.26
where the time goes:
time: 1320 us; the launch traced here: 1300 us
  local copies, waits for them, and re-layouts  496 us (38%)
  waiting for transfers between devices  273 us (21%)
  blocking collectives  170 us (13%)
  other arithmetic  168 us (13%)
  matrix products  145 us (11%)
  between operations  19.7 us (1%)
  loops' own time  18.5 us (1%)
    dynamic_update_slice x32, local copies, waits for them, and re-layouts, state_space(): lax.scan(jax.checkpoint(one_block), (state_init, prev_segment), inputs)  340 us
    reduce_scatter x1, waiting for transfers between devices, body(): lax.psum_scatter(grad_in_full, 'shard', scatter_dimension=0, tiled=True)  126 us
    unnamed x2, blocking collectives  71.5 us
    psum x1, blocking collectives, body(): head_sums = lax.psum((g_dt_bias, g_a_log, g_d_skip), ('replica', 'shard'))  44.8 us
    all_gather x2, waiting for transfers between devices, prefix(): lax.all_gather(part.astype(kind), axis)  43.8 us
    psum x1, waiting for transfers between devices, body(): lax.psum((part_in, part_out, part_conv, part_bias, part_norm, part_gate),...  42.9 us
    dynamic_slice x28, local copies, waits for them, and re-layouts, state_space(): lax.scan(jax.checkpoint(one_block), (state_init, prev_segment), inputs)  37.6 us
    unnamed x124, local copies, waits for them, and re-layouts  35.9 us
  transfers between devices with their start and end apart: 11, of which 8 were waited for; matrix products, arithmetic and copies ran while one was open for 40% of the time, Pallas kernels for 0%

commit v1 on v0

v1 whole, which is shorter than its diff:
```python
import jax
import jax.numpy as jnp
from jax import lax
from jax.experimental import pallas as pl
from jax.experimental.pallas import tpu as pltpu
from jax.sharding import PartitionSpec as P

H = 24
P_SIZE = 64
N = 128
KC = 4
SPAN = 256
DI = 1536
CONV = 1792


EPSILON = 1e-05
WRAP_IDS = 256


def passed_along(shard, axis, by):
    count = lax.axis_size(axis)
    pairs = [(i, i + by) for i in range(count) if 0 <= i + by < count]
    return lax.ppermute(shard, axis, pairs)


def rms_scale(values, gain_vec):
    return (
        values * lax.rsqrt(jnp.mean(values * values, axis=-1, keepdims=True) + EPSILON) * gain_vec
    )


def causal_conv(xbc_in, rim_in, weight_in, bias_in, segment_ids, rim_segments):
    width = weight_in.shape[0]
    length = xbc_in.shape[0]
    row_block = jnp.concatenate([rim_in, xbc_in], axis=0)
    seg_block = jnp.concatenate([rim_segments, segment_ids], axis=0)
    summed = jnp.zeros_like(xbc_in) + bias_in[None, :]
    for offset in range(width):
        kept_mask = (seg_block[offset : offset + length] == segment_ids).astype(jnp.float32)
        summed = (
            summed
            + weight_in[offset][None, :] * row_block[offset : offset + length] * kept_mask[:, None]
        )
    return jax.nn.silu(summed)


def log_decay(raw_in, bias_in, alog_in):
    step_size = jax.nn.softplus(raw_in + bias_in[None, :])
    return (step_size, -jnp.exp(alog_in)[None, :] * step_size)


def gated_norm(mixed_in, gate_in, gain_in):
    product = mixed_in * jax.nn.silu(gate_in)
    return (
        product
        * lax.rsqrt(jnp.mean(product * product, axis=-1, keepdims=True) + EPSILON)
        * gain_in[None, :]
    )


MASKED = -1e30
HIGH = lax.Precision.HIGHEST


def mm(a, b, dims):
    return lax.dot_general(
        a.astype(jnp.bfloat16),
        b.astype(jnp.bfloat16),
        (dims, ((), ())),
        preferred_element_type=jnp.float32,
    )


NN = ((1,), (0,))
NT = ((1,), (1,))
TN = ((0,), (0,))


def block_mask(segc_ref, segr_ref):
    span = segc_ref.shape[0]
    at = lax.broadcasted_iota(jnp.int32, (span, span), 0)
    of = lax.broadcasted_iota(jnp.int32, (span, span), 1)
    keep = (segc_ref[:, 0:1] == segr_ref[0:1, :]) & (at >= of)
    return jnp.where(keep, 0.0, MASKED)


def pair_columns(cols, first):
    lane = lax.broadcasted_iota(jnp.int32, (cols.shape[0], 2 * P_SIZE), 1)
    return jnp.where(lane < P_SIZE, cols[:, first : first + 1], cols[:, first + 1 : first + 2])


def forward_kernel(
    conv_ref, cols_ref, rows_ref, segc_ref, segr_ref, skip_ref,
    mixed_ref, enter_ref, final_ref, state, bias, scores,
):
    span = conv_ref.shape[0]
    pairs = cols_ref.shape[0]
    wide = 2 * P_SIZE

    @pl.when(pl.program_id(0) == 0)
    def _():
        state[...] = jnp.zeros_like(state)

    b_mat = conv_ref[:, DI : DI + N]
    c_mat = conv_ref[:, DI + N :]
    bias[...] = block_mask(segc_ref, segr_ref)
    scores[...] = mm(c_mat, b_mat, NT)
    enter_ref[0] = state[...]
    lane = lax.broadcasted_iota(jnp.int32, (span, wide), 1)

    @pl.loop(0, pairs)
    def _(j):
        at = pl.ds(pl.multiple_of(j * wide, wide), wide)
        cols = cols_ref[j]
        xs = conv_ref[:, at].astype(jnp.float32)
        x = xs * pair_columns(cols, 2)
        xb = x.astype(jnp.bfloat16)
        parts = []
        for a in range(2):
            gaps = cols[:, a : a + 1] - rows_ref[j, a : a + 1, :]
            w = jnp.exp(gaps + bias[...]) * scores[...]
            parts.append(mm(w, xb, NN))
        within = jnp.where(lane < P_SIZE, parts[0], parts[1])
        enter = pair_columns(cols, 4)
        old = state[at, :]
        from_state = mm(c_mat, old, NT) * enter
        mixed_ref[:, at] = within + from_state + skip_ref[:, at] * xs
        leave = pair_columns(cols, 6)
        sub = lax.broadcasted_iota(jnp.int32, (wide, N), 0)
        passing = jnp.where(sub < P_SIZE, cols[span - 1 :, 4:5], cols[span - 1 :, 5:6])
        state[at, :] = old * passing + mm(x * leave, b_mat, TN)

    final_ref[...] = state[...]


def backward_kernel(
    conv_ref, gmix_ref, cols_ref, rows_ref, segc_ref, segr_ref, skip_ref, enter_ref, gout_ref,
    gconv_ref, gcols_ref, grows_ref, gskip_ref, gstate, bias, scores, gscores, gbc,
):
    span = conv_ref.shape[0]
    pairs = cols_ref.shape[0]
    wide = 2 * P_SIZE

    @pl.when(pl.program_id(0) == 0)
    def _():
        gstate[...] = gout_ref[...]
        gskip_ref[...] = jnp.zeros_like(gskip_ref)

    b_mat = conv_ref[:, DI : DI + N]
    c_mat = conv_ref[:, DI + N :]
    bias[...] = block_mask(segc_ref, segr_ref)
    scores[...] = mm(c_mat, b_mat, NT)
    gscores[...] = jnp.zeros_like(gscores)
    gbc[...] = jnp.zeros_like(gbc)
    lane = lax.broadcasted_iota(jnp.int32, (span, wide), 1)
    low = lane < P_SIZE
    low_sub = lax.broadcasted_iota(jnp.int32, (wide, N), 0) < P_SIZE
    last = lax.broadcasted_iota(jnp.int32, (span, 1), 0) == span - 1
    lane8 = lax.broadcasted_iota(jnp.int32, (span, 8), 1)

    @pl.loop(0, pairs)
    def _(j):
        at = pl.ds(pl.multiple_of(j * wide, wide), wide)
        cols = cols_ref[j]
        xs = conv_ref[:, at].astype(jnp.float32)
        dt = pair_columns(cols, 2)
        x = xs * dt
        xb = x.astype(jnp.bfloat16)
        gy = gmix_ref[:, at]
        gyb = gy.astype(jnp.bfloat16)
        parts = []
        row_sums = []
        for a in range(2):
            gaps = cols[:, a : a + 1] - rows_ref[j, a : a + 1, :]
            e = jnp.exp(gaps + bias[...])
            w = e * scores[...]
            mine = low if a == 0 else jnp.logical_not(low)
            dw = mm(jnp.where(mine, gy, 0.0), xb, NT)
            gscores[...] += e * dw
            q = w * dw
            row_sums.append(jnp.sum(q, axis=1, keepdims=True))
            grows_ref[j, a : a + 1, :] = jnp.sum(q, axis=0, keepdims=True)
            parts.append(mm(w, gyb, TN))
        gx = jnp.where(low, parts[0], parts[1])
        enter = pair_columns(cols, 4)
        leave = pair_columns(cols, 6)
        old = enter_ref[0, at, :]
        late = gstate[at, :]
        gye = gy * enter
        from_state = mm(c_mat, old, NT)
        gx_late = mm(b_mat, late, NT) * leave
        gbc[:, N:] += mm(gye, old, NN)
        gbc[:, :N] += mm(x * leave, late, NN)
        gx = gx + gx_late
        late_term = x * gx_late
        v1 = gye * from_state - late_term
        v2 = gx * xs
        passing = jnp.where(low_sub, cols[span - 1 :, 4:5], cols[span - 1 :, 5:6])
        through = late * passing
        kept = jnp.sum(through * old, axis=1, keepdims=True)
        ends = jnp.sum(late_term, axis=0, keepdims=True)
        low_row = lax.broadcasted_iota(jnp.int32, (1, wide), 1) < P_SIZE
        out = jnp.zeros((span, 8), jnp.float32)
        for a in range(2):
            mine = low if a == 0 else jnp.logical_not(low)
            mine_row = low_row if a == 0 else jnp.logical_not(low_row)
            tail = jnp.sum(jnp.where(mine_row, ends, 0.0), axis=1, keepdims=True)
            tail = tail + jnp.sum(
                kept[a * P_SIZE : (a + 1) * P_SIZE], axis=0, keepdims=True
            )
            gcum = row_sums[a] + jnp.sum(jnp.where(mine, v1, 0.0), axis=1, keepdims=True)
            gcum = gcum + jnp.where(last, tail, 0.0)
            gdt = jnp.sum(jnp.where(mine, v2, 0.0), axis=1, keepdims=True)
            out = jnp.where(lane8 == a, gcum, out)
            out = jnp.where(lane8 == 2 + a, gdt, out)
        gcols_ref[j] = out
        gskip_ref[:, at] += jnp.sum(gy * xs, axis=0, keepdims=True)
        gconv_ref[:, at] = gx * dt + skip_ref[:, at] * gy
        gstate[at, :] = through + mm(gye, c_mat, TN)

    gs = gscores[...].astype(jnp.bfloat16)
    gconv_ref[:, DI : DI + N] = gbc[:, :N] + mm(gs, c_mat, TN)
    gconv_ref[:, DI + N :] = gbc[:, N:] + mm(gs, b_mat, NN)


def scan_specs(count, order):
    pairs = H // 2
    return dict(
        conv=pl.BlockSpec((SPAN, CONV), lambda i: (order(i), 0)),
        mix=pl.BlockSpec((SPAN, DI), lambda i: (order(i), 0)),
        cols=pl.BlockSpec((pairs, SPAN, 8), lambda i: (0, order(i), 0)),
        rows=pl.BlockSpec((pairs, 2, SPAN), lambda i: (0, 0, order(i))),
        segc=pl.BlockSpec((SPAN, 1), lambda i: (order(i), 0)),
        segr=pl.BlockSpec((1, SPAN), lambda i: (0, order(i))),
        skip=pl.BlockSpec((1, DI), lambda i: (0, 0)),
        state=pl.BlockSpec((DI, N), lambda i: (0, 0)),
        states=pl.BlockSpec((1, DI, N), lambda i: (order(i), 0, 0)),
    )


def scan_forward(conv_b, cols, rows, segc, segr, skip):
    length = conv_b.shape[0]
    count = length // SPAN
    s = scan_specs(count, lambda i: i)
    f32 = jnp.float32
    return pl.pallas_call(
        forward_kernel,
        grid=(count,),
        in_specs=[s["conv"], s["cols"], s["rows"], s["segc"], s["segr"], s["skip"]],
        out_specs=[s["mix"], s["states"], s["state"]],
        out_shape=[
            jax.ShapeDtypeStruct((length, DI), f32),
            jax.ShapeDtypeStruct((count, DI, N), f32),
            jax.ShapeDtypeStruct((DI, N), f32),
        ],
        scratch_shapes=[
            pltpu.VMEM((DI, N), f32),
            pltpu.VMEM((SPAN, SPAN), f32),
            pltpu.VMEM((SPAN, SPAN), f32),
        ],
        compiler_params=pltpu.CompilerParams(vmem_limit_bytes=48 << 20),
    )(conv_b, cols, rows, segc, segr, skip)


def scan_backward(conv_b, g_mixed, cols, rows, segc, segr, skip, states, g_out):
    length = conv_b.shape[0]
    count = length // SPAN
    s = scan_specs(count, lambda i: count - 1 - i)
    f32 = jnp.float32
    return pl.pallas_call(
        backward_kernel,
        grid=(count,),
        in_specs=[
            s["conv"], s["mix"], s["cols"], s["rows"], s["segc"], s["segr"], s["skip"],
            s["states"], s["state"],
        ],
        out_specs=[s["conv"], s["cols"], s["rows"], s["skip"]],
        out_shape=[
            jax.ShapeDtypeStruct((length, CONV), f32),
            jax.ShapeDtypeStruct(cols.shape, f32),
            jax.ShapeDtypeStruct(rows.shape, f32),
            jax.ShapeDtypeStruct((1, DI), f32),
        ],
        scratch_shapes=[
            pltpu.VMEM((DI, N), f32),
            pltpu.VMEM((SPAN, SPAN), f32),
            pltpu.VMEM((SPAN, SPAN), f32),
            pltpu.VMEM((SPAN, SPAN), f32),
            pltpu.VMEM((SPAN, 2 * N), f32),
        ],
        compiler_params=pltpu.CompilerParams(vmem_limit_bytes=48 << 20),
    )(conv_b, g_mixed, cols, rows, segc, segr, skip, states, g_out)


def carried(state, gain, reverse):
    count, mine = (lax.axis_size("shard"), lax.axis_index("shard"))
    sent = jnp.concatenate(
        [state, jnp.pad(gain[None, :], ((0, 15), (0, N - H)))], axis=0
    ).astype(jnp.bfloat16)
    everything = lax.all_gather(sent, "shard")
    gains = everything[:, DI, :H].astype(jnp.float32)
    weights = [None] * count
    run = jnp.ones((H,), jnp.float32)
    for k in range(count) if reverse else reversed(range(count)):
        counts = k > mine if reverse else k < mine
        weights[k] = jnp.where(counts, run, 0.0)
        run = jnp.where(counts, run * gains[k], run)
    total = jnp.zeros((H, P_SIZE, N), jnp.float32)
    for k in range(count):
        total = total + weights[k][:, None, None] * everything[k, :DI].reshape(
            H, P_SIZE, N
        ).astype(jnp.float32)
    return total.reshape(DI, N)


def gather_params(w_in, w_out, conv_w, conv_b, norm_gain, gate_gain):
    parts = lax.axis_size("replica")
    mine = lax.axis_index("replica")

    def whole(w):
        rows = w.shape[0] // parts
        part = lax.dynamic_slice_in_dim(w, mine * rows, rows, 0)
        return lax.all_gather(part, ("shard", "replica"), axis=0, tiled=True)

    small = jnp.concatenate([conv_w.reshape(-1), conv_b, norm_gain, gate_gain])
    small = lax.all_gather(small, "shard", axis=0)
    count = small.shape[0]
    a = conv_w.size
    b = a + conv_b.size
    c = b + norm_gain.size
    full_conv = small[:, :a].reshape(count, KC, -1).transpose(1, 0, 2).reshape(KC, -1)
    return (
        whole(w_in),
        whole(w_out),
        full_conv.astype(jnp.float32),
        small[:, a:b].reshape(-1).astype(jnp.float32),
        small[:, b:c].reshape(-1).astype(jnp.float32),
        small[:, c:].reshape(-1).astype(jnp.float32),
    )


def owned_sum(g):
    part = lax.psum_scatter(
        g.astype(jnp.bfloat16), ("shard", "replica"), scatter_dimension=0, tiled=True
    )
    return lax.all_gather(part, "replica", axis=0, tiled=True).astype(jnp.float32)


def body(
    tokens,
    segment,
    norm_gain,
    w_in,
    conv_w,
    conv_b,
    dt_bias,
    a_log,
    d_skip,
    gate_gain,
    w_out,
    cotangent,
):
    full_in, full_out, full_conv, full_bias, full_norm, full_gate = gather_params(
        w_in, w_out, conv_w, conv_b, norm_gain, gate_gain
    )
    rim_len = KC - 1
    wrapped = segment % WRAP_IDS
    tok_f = tokens.astype(jnp.float32)
    count = tokens.shape[0]
    blocks = count // SPAN

    def norm_piece(tok_in, gain_in):
        return rms_scale(tok_in, gain_in[None, :])

    normed, norm_pull = jax.vjp(norm_piece, tok_f, full_norm)
    normed_b = normed.astype(jnp.bfloat16)
    projected = jnp.dot(normed_b, full_in, preferred_element_type=jnp.float32).astype(jnp.bfloat16)
    xbc_b = projected[:, DI : DI + CONV]
    rim = jnp.concatenate(
        [
            xbc_b[-rim_len:],
            jnp.broadcast_to(wrapped[-rim_len:, None].astype(jnp.bfloat16), (rim_len, N)),
        ],
        axis=1,
    )
    rim = passed_along(rim, "shard", 1)
    rim_rows = rim[:, :CONV]
    prev_segs = rim[:, CONV].astype(jnp.int32)
    prev_last = jnp.where(lax.axis_index("shard") == 0, 0, prev_segs[-1])
    xbc_f = xbc_b.astype(jnp.float32)
    rim_f = rim_rows.astype(jnp.float32)
    gate_z = projected[:, :DI].astype(jnp.float32)
    dt_raw = projected[:, DI + CONV :].astype(jnp.float32)

    def conv_piece(xbc_in, rim_in, weight_in, bias_in):
        return causal_conv(xbc_in, rim_in, weight_in, bias_in, wrapped, prev_segs)

    conv_out, conv_pull = jax.vjp(conv_piece, xbc_f, rim_f, full_conv, full_bias)
    conv_bf = conv_out.astype(jnp.bfloat16)

    step, decay = log_decay(dt_raw, dt_bias, a_log)
    decay_blocks = decay.reshape(blocks, SPAN, H)
    lower = jnp.tril(jnp.ones((SPAN, SPAN), jnp.float32))
    cum_blocks = jnp.einsum("ts,bsh->bth", lower, decay_blocks, precision=HIGH)
    seg_blocks = wrapped.reshape(blocks, SPAN)
    ends = seg_blocks[:, -1]
    before = jnp.concatenate([prev_last[None], ends[:-1]])
    at_last = cum_blocks[:, -1:]
    enter = jnp.exp(cum_blocks) * (seg_blocks == before[:, None]).astype(jnp.float32)[:, :, None]
    leave = (
        jnp.exp(at_last - cum_blocks)
        * (seg_blocks == ends[:, None]).astype(jnp.float32)[:, :, None]
    )
    before_sum = [jnp.zeros((H,), jnp.float32)]
    for b in range(blocks):
        before_sum.append(before_sum[-1] + cum_blocks[b, -1])
    base = jnp.stack(before_sum[:-1])
    running = (
        jnp.exp(cum_blocks + base[:, None, :]).reshape(count, H)
        * (wrapped == prev_last).astype(jnp.float32)[:, None]
    )
    carry_gain = running[-1]
    entering_gain = jnp.concatenate(
        [jnp.ones((1, H), jnp.float32), running.reshape(blocks, SPAN, H)[:-1, -1]]
    )

    pairs = H // 2
    cols = jnp.stack(
        [cum_blocks.reshape(count, H), step, enter.reshape(count, H), leave.reshape(count, H)],
        axis=1,
    )
    cols = cols.reshape(count, 4, pairs, 2).transpose(2, 0, 1, 3).reshape(pairs, count, 8)
    rows = cum_blocks.reshape(count, pairs, 2).transpose(1, 2, 0)
    segc = wrapped[:, None]
    segr = wrapped[None, :]
    skip = jnp.repeat(d_skip, P_SIZE)[None, :]

    local_mixed, local_states, local_state = scan_forward(conv_bf, cols, rows, segc, segr, skip)
    state_in = carried(local_state, carry_gain, False)
    c_mat = conv_bf[:, DI + N :]
    running_wide = jnp.repeat(running, P_SIZE, axis=1)
    mixed_out = local_mixed + mm(c_mat, state_in, NT) * running_wide
    gated_out, gate_pull = jax.vjp(gated_norm, mixed_out, gate_z, full_gate)
    gated_b = gated_out.astype(jnp.bfloat16)
    branch = jnp.dot(gated_b, full_out, preferred_element_type=jnp.float32)
    block_out = (tok_f + branch).astype(jnp.bfloat16)

    g_gated = mm(cotangent, full_out, NT)
    grad_out_full = mm(gated_b, cotangent, TN)
    part_out = owned_sum(grad_out_full)
    g_mixed, g_gate_z, g_gate_gain = gate_pull(g_gated)
    seed_grad = mm(g_mixed * running_wide, c_mat, TN)
    state_out_grad = carried(seed_grad, carry_gain, True)
    states = (
        local_states
        + jnp.repeat(entering_gain, P_SIZE, axis=1)[:, :, None] * state_in[None]
    )
    g_conv, g_cols, g_rows, g_skip = scan_backward(
        conv_bf, g_mixed, cols, rows, segc, segr, skip, states, state_out_grad
    )
    g_d_skip = g_skip.reshape(H, P_SIZE).sum(1)
    g_cols = g_cols[:, :, :4].reshape(pairs, count, 2, 2).transpose(2, 1, 0, 3)
    g_cols = g_cols.reshape(2, count, H)
    g_cum = g_cols[0] - g_rows.reshape(H, count).T
    g_decay = jnp.einsum(
        "ts,bth->bsh", lower, g_cum.reshape(blocks, SPAN, H), precision=HIGH
    ).reshape(count, H)
    g_step = g_cols[1] - jnp.exp(a_log)[None, :] * g_decay
    g_a_log = (g_decay * decay).sum(0)
    g_dt_raw = g_step * jax.nn.sigmoid(dt_raw + dt_bias[None, :])
    g_dt_bias = g_dt_raw.sum(0)

    g_xbc, g_rim, g_conv_w, g_conv_b = conv_pull(g_conv)
    from_next = passed_along(g_rim, "shard", -1)
    g_xbc = g_xbc + jnp.pad(from_next, ((count - rim_len, 0), (0, 0)))
    g_projected = jnp.concatenate([g_gate_z, g_xbc, g_dt_raw], axis=1).astype(jnp.bfloat16)
    grad_in_full = mm(normed_b, g_projected, TN)
    part_in = owned_sum(grad_in_full)
    g_normed = mm(g_projected, full_in, NT)
    g_tokens, g_norm_gain = norm_pull(g_normed)
    grad_tokens = cotangent.astype(jnp.float32) + g_tokens

    flat = jnp.concatenate(
        [g_conv_w.reshape(-1), g_conv_b, g_norm_gain, g_gate_gain, g_dt_bias, g_a_log, g_d_skip]
    )
    width = flat.size
    flat = jnp.pad(flat, (0, -width % 1024)).reshape(-1, N)
    flat = lax.psum(flat, ("replica", "shard")).reshape(-1)
    cuts = [0]
    for g in (g_conv_w, g_conv_b, g_norm_gain, g_gate_gain, g_dt_bias, g_a_log, g_d_skip):
        cuts.append(cuts[-1] + g.size)
    piece = [flat[a:b] for a, b in zip(cuts, cuts[1:])]
    at = lax.axis_index("shard")

    def own(v, like):
        return lax.dynamic_slice_in_dim(v, at * like.shape[-1], like.shape[-1], v.ndim - 1)

    return (
        block_out,
        grad_tokens,
        own(piece[2], norm_gain),
        part_in,
        own(piece[0].reshape(KC, -1), conv_w),
        own(piece[1], conv_b),
        piece[4],
        piece[5],
        piece[6],
        own(piece[3], gate_gain),
        part_out,
    )


def solution(mesh):
    in_specs = (
        P(("replica", "shard"), None),
        P(("replica", "shard")),
        P("shard"),
        P("shard", None),
        P(None, "shard"),
        P("shard"),
        P(),
        P(),
        P(),
        P("shard"),
        P("shard", None),
        P(("replica", "shard"), None),
    )
    out_specs = (
        P(("replica", "shard"), None),
        P(("replica", "shard"), None),
        P("shard"),
        P("shard", None),
        P(None, "shard"),
        P("shard"),
        P(),
        P(),
        P(),
        P("shard"),
        P("shard", None),
    )
    return jax.shard_map(body, mesh=mesh, in_specs=in_specs, out_specs=out_specs, check_vma=False)
```

time: 1320 us -> 643 us (0.49)
  local copies, waits for them, and re-layouts: 496 us -> 44.1 us
  Pallas kernels: 0 us -> 113 us
  blocking collectives: 170 us -> 89.1 us
  matrix products: 145 us -> 69.1 us
  waiting for transfers between devices: 273 us -> 198 us
  other arithmetic: 168 us -> 100 us
  loops' own time: 18.5 us -> 0 us
    dynamic_update_slice x32 -> x0, local copies, waits for them, and re-layouts: 340 us -> none  [state_space(): lax.scan(jax.checkpoint(one_block), (state_init, prev_segment), inputs)]
    reduce_scatter x2 -> x1, waiting for transfers between devices: 126 us -> 0.01 us  [owned_sum(): lax.psum_scatter(g.astype(jnp.bfloat16), ('shard', 'replica'), scatter_di...]
    pallas_call x0 -> x2, Pallas kernels: none -> 113 us  [the longest x1 83.4 us: scan_backward(): pl.pallas_call(backward_kernel, grid=(count,), in_specs=[s['conv'], s['mi...]
    all_gather x4, waiting for transfers between devices: 81.1 us -> 169 us  [the longest x2 94.1 us: carried(): everything = lax.all_gather(sent, 'shard')]
    dot_general x66 -> x8, matrix products: 128 us -> 52.7 us  [the longest x6 51.4 us: mm(): lax.dot_general(a.astype(jnp.bfloat16), b.astype(jnp.bfloat16), (dims, ((...]
    unnamed x2 -> x0, blocking collectives: 71.5 us -> none
    psum x1 -> x0, waiting for transfers between devices: 42.9 us -> none  [body(): lax.psum((part_in, part_out, part_conv, part_bias, part_norm, part_gate),...]
    dynamic_slice x28 -> x6, local copies, waits for them, and re-layouts: 37.6 us -> 4.73 us  [the longest x4 2.53 us: own(): lax.dynamic_slice_in_dim(v, at * like.shape[-1], like.shape[-1], v.ndim - 1)]
  transfers between devices with their start and end apart: 11 -> 8, of which waited for: 8 -> 5; matrix products, arithmetic and copies ran while one was open for 40% -> 22% of each run, Pallas kernels for 0% -> 13%
where the time goes in v1:
time: 643 us; the launch traced here: 635 us
  waiting for transfers between devices  198 us (31%)
  Pallas kernels  113 us (18%)
  other arithmetic  100 us (16%)
  blocking collectives  89.1 us (14%)
  matrix products  69.1 us (11%)
  local copies, waits for them, and re-layouts  44.1 us (7%)
  between operations  15.9 us (2%)
    all_gather x2, waiting for transfers between devices, carried(): everything = lax.all_gather(sent, 'shard')  94.1 us
    pallas_call x1, Pallas kernels, scan_backward(): pl.pallas_call(backward_kernel, grid=(count,), in_specs=[s['conv'], s['mi...  83.4 us
    all_gather x2, waiting for transfers between devices, whole(): return lax.all_gather(part, ('shard', 'replica'), axis=0, tiled=True)  75.3 us
    dot_general x6, matrix products, mm(): lax.dot_general(a.astype(jnp.bfloat16), b.astype(jnp.bfloat16), (dims, ((...  51.4 us
    psum x1, blocking collectives, body(): flat = lax.psum(flat, ('replica', 'shard')).reshape(-1)  42.5 us
    all_gather x1, blocking collectives, gather_params(): small = lax.all_gather(small, 'shard', axis=0)  32.5 us
    pallas_call x1, Pallas kernels, scan_forward(): pl.pallas_call(forward_kernel, grid=(count,), in_specs=[s['conv'], s['col...  30.1 us
    unnamed x7, waiting for transfers between devices  28.2 us
  transfers between devices with their start and end apart: 8, of which 5 were waited for; matrix products, arithmetic and copies ran while one was open for 22% of the time, Pallas kernels for 13%

profile of v1, /device:TPU:0, one launch (start us, length us, event | category | flops | bytes accessed | tf_op | source)
XLA Modules:
  0.0 635.2 jit_solution(12028206517131746820)
XLA Ops:
  13.5 32.5 %all-gather.1 = bf16[8,1,1408]{2,1,0:T(2,128)(2,1)S(1)} all-gather(bf16[1,1,1408]{2,1,0:T(2,128)(2,1)S(1)} %reshape.726), channel_id=2, replica_groups=mesh['replica'=4,'shard'=8] {'shard'}, dimensions={0}, use_global_device_ids=true | all-gather | bytes 25344 | tf_op jit(solution)/shard_map/all_gather | solution.py:327
  49.8 30.1 %all-gather.7.cloned.1.call-done = bf16[768,3352]{1,0:T(8,128)(2,1)} async-done(((bf16[24,3352]{1,0:T(8,128)(2,1)}), bf16[768,3352]{1,0:T(8,128)(2,1)}) %all-gather.7.cloned.1.call-update) | async-done | bytes 5148688 | tf_op jit(solution)/shard_map/all_gather | solution.py:324
  79.9 9.1 %convolution_convert_fusion = bf16[1024,3352]{1,0:T(8,128)(2,1)S(1)} fusion(bf16[768,3352]{1,0:T(8,128)(2,1)} %all-gather.7.cloned.1.call-done, bf16[1024,768]{1,0:T(8,128)(2,1)} %param.12, f32[768]{0:T(1024)S(1)} %reshape.707, f32[1024]{0:T(1024)S(1)} %fusion.101), kind=kOutput, calls=%fused_computation.8 | convolution fusion | flops 5278818304 | bytes 13593600 | tf_op jit(solution)/shard_map/dot_general | solution.py:378
  105.5 19.6 %multiply_convert_fusion = (bf16[1024,1792]{1,0:T(8,128)(2,1)}, f32[1024,1792]{1,0:T(8,128)}) fusion(f32[1024,1792]{1,0:T(8,128)} %slice_convert_fusion, f32[1792]{0:T(1024)S(1)} %mul.802, f32[1024]{0:T(1024)S(1)} %get-tuple-element.80, f32[3,1792]{1,0:T(4,128)S(1)} %slice_convert_fusion.1, f32[1792]{0:T(1024)S(1)} %mul.797, f32[1024]{0:T(1024)S(1)} %get-tuple-element.81, ...), kind=kLoop, calls=%fused_computation.21 | loop fusion | flops 34865152 | bytes 18419712 | tf_op jit(solution)/shard_map/convert_element_type | solution.py:400
  125.0 30.1 %shard_map.203 = (f32[1024,1536]{1,0:T(8,128)}, f32[4,1536,128]{2,1,0:T(8,128)S(1)}, f32[1536,128]{1,0:T(8,128)S(1)}) custom-call(bf16[1024,1792]{1,0:T(8,128)(2,1)} %get-tuple-element.58.conv_ref, f32[12,1024,8]{2,1,0:T(8,128)} %copy.105.cols_ref, f32[12,2,1024]{2,1,0:T(2,128)S(1)} %bitcast.313, s32[1024,1]{1,0:T(8,128)S(1)} %copy.106.segc_ref, ...), custom_call_target="tpu_custom_call" | custom-call | tf_op jit(solution)/shard_map/pallas_call | solution.py:247
  163.2 6.6 %copy.109 = f32[1024,1536]{1,0:T(8,128)} copy(f32[1024,1536]{0,1:T(8,128)} %bitcast.320) | data formatting | bytes 12582912 | tf_op jit(solution)/shard_map/reshape | solution.py:442
  169.8 48.5 %all-gather.9.cloned.1.call-done = bf16[8,1552,128]{2,1,0:T(8,128)(2,1)} async-done(((bf16[1,1552,128]{2,1,0:T(8,128)(2,1)}), bf16[8,1552,128]{2,1,0:T(8,128)(2,1)}) %all-gather.9.cloned.1.call-update) | async-done | bytes 3178512 | tf_op jit(solution)/shard_map/all_gather | solution.py:301
  220.1 12.5 %multiply_reduce_fusion.5 = (f32[1024]{0:T(1024)S(1)}, f32[1024,1536]{1,0:T(8,128)}, f32[1024,1536]{1,0:T(8,128)}) fusion(bf16[1024,3352]{1,0:T(8,128)(2,1)} %copy-done.8, f32[1024,1536]{1,0:T(8,128)} %get-tuple-element.18, f32[1024,1536]{1,0:T(8,128)} %copy.109, f32[]{:T(128)S(6)} %select_n.469, f32[1536]{0:T(1024)S(1)} %mul.845, f32[1536]{0:T(1024)S(1)} %mul.841, ...), kind=kOutput, calls=%fused_computation.41 | convolution fusion | flops 423099392 | bytes 31766532 | tf_op jit(solution)/shard_map/dot_general | solution.py:67
  232.6 45.1 %all-gather.11.cloned.1.call-done = bf16[1536,768]{1,0:T(8,128)(2,1)} async-done(((bf16[48,768]{1,0:T(8,128)(2,1)}), bf16[1536,768]{1,0:T(8,128)(2,1)}) %all-gather.11.cloned.1.call-update) | async-done | bytes 2359312 | tf_op jit(solution)/shard_map/all_gather | solution.py:324
  277.8 7.7 %fusion.11 = (f32[1536]{0:T(1024)S(1)}, f32[1024]{0:T(1024)S(1)}, f32[1536,1024]{0,1:T(8,128)}) fusion(f32[1024,1536]{1,0:T(8,128)} %get-tuple-element.51, f32[1024]{0:T(1024)S(1)} %fusion.102, f32[1536]{0:T(1024)S(1)} %reshape.716, bf16[1536,768]{1,0:T(8,128)(2,1)} %all-gather.11.cloned.1.call-done, bf16[1024,768]{1,0:T(8,128)(2,1)S(1)} %copy-done.13), kind=kOutput, calls=%fused_computation.37 | convolution fusion | flops 2425353728 | bytes 16535552 | tf_op jit(solution)/shard_map/dot_general | solution.py:67
  285.4 9.4 %fusion.10 = (bf16[1024,1536]{1,0:T(8,128)(2,1)}, f32[1024,1536]{1,0:T(8,128)S(1)}) fusion(f32[1024,1536]{1,0:T(8,128)} %get-tuple-element.95, f32[1024,1536]{1,0:T(8,128)S(1)} %copy-done.9, f32[1024]{0:T(1024)S(1)} %multiply_multiply_fusion.4, f32[1536,1024]{0,1:T(8,128)} %get-tuple-element.96, f32[1536]{0:T(1024)S(1)} %reshape.716, f32[1024]{0:T(1024)S(1)} %fusion.102, ...), kind=kLoop, calls=%fused_computation.34 | loop fusion | flops 29884416 | bytes 31471616 | tf_op jit(solution)/shard_map/convert.19
  299.4 7.1 %convolution_convert_fusion.2 = bf16[1536,768]{1,0:T(8,128)(2,1)} fusion(bf16[1024,768]{1,0:T(8,128)(2,1)S(1)} %copy-done.13, f32[1024,1536]{1,0:T(8,128)} %get-tuple-element.51, f32[1536]{0:T(1024)S(1)} %reshape.716, f32[1024]{0:T(1024)S(1)} %fusion.102), kind=kOutput, calls=%fused_computation.53 | convolution fusion | flops 2421817344 | bytes 10233856 | tf_op jit(solution)/shard_map/dot_general | solution.py:67
  312.9 45.6 %all-gather.13.cloned.1.call-done = bf16[8,1552,128]{2,1,0:T(8,128)(2,1)} async-done(((bf16[1,1552,128]{2,1,0:T(8,128)(2,1)}), bf16[8,1552,128]{2,1,0:T(8,128)(2,1)}) %all-gather.13.cloned.1.call-update) | async-done | bytes 3178512 | tf_op jit(solution)/shard_map/all_gather | solution.py:301
  365.2 83.4 %shard_map.204 = (f32[1024,1792]{1,0:T(8,128)}, f32[12,1024,8]{2,1,0:T(8,128)}, f32[12,2,1024]{2,1,0:T(2,128)S(1)}, f32[1,1536]{1,0:T(1,128)S(1)}) custom-call(bf16[1024,1792]{1,0:T(8,128)(2,1)} %get-tuple-element.58.conv_ref, f32[1024,1536]{1,0:T(8,128)} %copy-done.7, f32[12,1024,8]{2,1,0:T(8,128)} %copy.105.cols_ref, f32[12,2,1024]{2,1,0:T(2,128)S(1)} %bitcast.314, ...), custom_call_target="tpu_custom_call" | custom-call | tf_op jit(solution)/shard_map/pallas_call | solution.py:271
  453.7 20.2 %multiply_reduce_fusion.2 = (f32[1792]{0:T(1024)S(1)}, f32[1792]{0:T(1024)S(1)}, f32[1792]{0:T(1024)S(1)}, f32[1792]{0:T(1024)S(1)}, f32[1792]{0:T(1024)S(1)}, /*index=5*/f32[1024,1792]{1,0:T(8,128)}) fusion(f32[1024,1792]{1,0:T(8,128)} %slice_convert_fusion, f32[3,1792]{1,0:T(4,128)S(1)} %slice_convert_fusion.1, f32[1024]{0:T(1024)S(1)} %get-tuple-element.80, ...), kind=kLoop, calls=%fused_computation.19 | loop fusion | flops 45866240 | bytes 33099776 | tf_op jit(solution)/shard_map/transpose(jvp())/reduce_sum | solution.py:43
  473.9 8.4 %broadcast_multiply_fusion = (f32[1024,1792]{1,0:T(8,128)S(1)}, f32[1024,1792]{1,0:T(8,128)S(1)}, f32[1024,1792]{1,0:T(8,128)}, f32[1024,1792]{1,0:T(8,128)}) fusion(f32[1024,1792]{1,0:T(8,128)} %get-tuple-element.43, f32[1792]{0:T(1024)S(1)} %mul.802, f32[1024]{0:T(1024)S(1)} %get-tuple-element.79, f32[1792]{0:T(1024)S(1)} %mul.781, ...), kind=kLoop, calls=%fused_computation.52 | loop fusion | flops 12845056 | bytes 36741120 | tf_op jit(solution)/shard_map/transpose(jvp())/mul | solution.py:43
  489.5 10.5 %pad_add_fusion = f32[1027,1792]{1,0:T(8,128)S(1)} fusion(f32[1024,1792]{1,0:T(8,128)} %copy-done.6, f32[1024,1792]{1,0:T(8,128)} %get-tuple-element.65, f32[1024,1792]{1,0:T(8,128)} %get-tuple-element.66, f32[1024,1792]{1,0:T(8,128)} %copy-done.5), kind=kLoop, calls=%fused_computation.9 | loop fusion | flops 5521152 | bytes 36721664 | tf_op jit(solution)/shard_map/transpose(jvp())/add_any | solution.py:43
  504.2 9.5 %convolution_convert_fusion.1 = bf16[768,3352]{1,0:T(8,128)(2,1)} fusion(bf16[1024,24]{1,0:T(8,128)(2,1)S(1)} %get-tuple-element.42, bf16[1024,1792]{1,0:T(8,128)(2,1)S(1)} %fusion.4, bf16[1024,1536]{1,0:T(8,128)(2,1)S(1)} %copy-done.12, bf16[1024,768]{1,0:T(8,128)(2,1)S(1)} %copy-done.10, f32[768]{0:T(1024)S(1)} %reshape.707, f32[1024]{0:T(1024)S(1)} %fusion.101), kind=kOutput, calls=%fused_computation.28 | convolution fusion | flops 5298554880 | bytes 13593600 | tf_op jit(solution)/shard_map/dot_general | solution.py:67
  513.7 7.3 %fusion.18 = bf16[1024,768]{1,0:T(8,128)(2,1)} fusion(bf16[1024,768]{1,0:T(8,128)(2,1)S(1)} %copy-done.10, bf16[1536,768]{1,0:T(8,128)(2,1)} %all-gather.11.cloned.1.call-done, f32[1024,1536]{1,0:T(8,128)} %get-tuple-element.51, f32[1536]{0:T(1024)S(1)} %reshape.716, f32[1024]{0:T(1024)S(1)} %fusion.102), kind=kOutput, calls=%fused_computation.58 | convolution fusion | flops 2422996992 | bytes 11806720 | tf_op jit(solution)/shard_map/dot_general | solution.py:446
  521.0 6.1 all_gather.33
  528.3 11.6 %fusion.15 = (f32[768]{0:T(1024)S(1)}, f32[1024]{0:T(1024)S(1)}, f32[1024,768]{1,0:T(8,128)}) fusion(bf16[1024,768]{1,0:T(8,128)(2,1)S(1)} %copy-done.10, f32[1024]{0:T(1024)S(1)} %fusion.101, f32[768]{0:T(1024)S(1)} %reshape.707, bf16[768,3352]{1,0:T(8,128)(2,1)} %all-gather.7.cloned.1.call-done, bf16[1024,24]{1,0:T(8,128)(2,1)S(1)} %get-tuple-element.42, ...), kind=kOutput, calls=%fused_computation.55 | convolution fusion | flops 5298337792 | bytes 16746496 | tf_op jit(solution)/shard_map/dot_general | solution.py:67
  540.0 42.5 %psum.7 = f32[96,128]{1,0:T(8,128)S(1)} all-reduce(f32[96,128]{1,0:T(8,128)S(1)} %pad_bitcast_fusion), channel_id=1, replica_groups=mesh['replica'=4,'shard'=8] {'replica','shard'}, use_global_device_ids=true, to_apply=%region_14.15 | all-reduce | flops 12288 | bytes 98304 | tf_op jit(solution)/shard_map/psum | solution.py:489
  590.6 28.1 %reduce-scatter.7.cloned.1.call-done = bf16[24,3352]{1,0:T(8,128)(2,1)} async-done(((bf16[768,3352]{1,0:T(8,128)(2,1)}), bf16[24,3352]{1,0:T(8,128)(2,1)}) %reduce-scatter.7.cloned.1.call-update) | async-done | bytes 160912
  618.7 8.1 %all_gather.32 = bf16[96,3352]{1,0:T(8,128)(2,1)S(1)} all-gather(bf16[24,3352]{1,0:T(8,128)(2,1)} %reduce-scatter.7.cloned.1.call-done), channel_id=1, replica_groups=mesh['replica'=4,'shard'=8] {'replica'}, dimensions={0}, use_global_device_ids=true | all-gather | bytes 804480 | tf_op jit(solution)/shard_map/all_gather | solution.py:347
  (216 shorter events, 79.7 us)
Async XLA Ops:
  7.2 72.7 %all-gather.7.cloned.1.call-start = ((), (), s32[]{:S(2)}) async-start(), calls=%async_computation.2 | async-start | bytes 5474304 | tf_op jit(solution)/shard_map/all_gather | solution.py:324
  9.0 209.3 %all-gather.9.cloned.1.call-start = ((), (), s32[]{:S(2)}) async-start(), calls=%async_computation.3 | async-start | bytes 3575808 | tf_op jit(solution)/shard_map/all_gather | solution.py:301
  46.9 78.1 %copy-start.2 = (s32[1024,1]{1,0:T(8,128)}, s32[1024,1]{1,0:T(8,128)S(1)}, u32[]{:S(2)}) copy-start(s32[1024,1]{1,0:T(8,128)S(1)} %copy.106.segc_ref) | copy-start | bytes 12292
  49.1 30.8 %copy-start.14 = (f32[1024]{0:T(1024)}, f32[1024]{0:T(1024)S(1)}, u32[]{:S(2)}) copy-start(f32[1024]{0:T(1024)S(1)} %fusion.17) | copy-start | bytes 12292
  89.0 8.7 %copy-start.8 = (bf16[1024,3352]{1,0:T(8,128)(2,1)}, bf16[1024,3352]{1,0:T(8,128)(2,1)S(1)}, u32[]{:S(2)}) copy-start(bf16[1024,3352]{1,0:T(8,128)(2,1)S(1)} %convolution_convert_fusion) | copy-start | bytes 20594692
  89.0 7.3 %copy-start.17 = (f32[24]{0:T(128)S(1)}, f32[24]{0:T(128)}, u32[]{:S(2)}) copy-start(f32[24]{0:T(128)} %param.18) | copy-start | bytes 292
  89.1 10.8 %copy-start.16 = (s32[1024]{0:T(1024)S(1)}, s32[1024]{0:T(1024)}, u32[]{:S(2)}) copy-start(s32[1024]{0:T(1024)} %param.13) | copy-start | bytes 12292
  93.1 5.6 collective-permute-start
  157.6 120.1 %all-gather.11.cloned.1.call-start = ((), (), s32[]{:S(2)}) async-start(), calls=%async_computation.4 | async-start | bytes 2433024 | tf_op jit(solution)/shard_map/all_gather | solution.py:324
  159.2 199.3 %all-gather.13.cloned.1.call-start = ((), (), s32[]{:S(2)}) async-start(), calls=%async_computation.5 | async-start | bytes 3575808 | tf_op jit(solution)/shard_map/all_gather | solution.py:301
  220.1 57.7 %copy-start.13 = (bf16[1024,768]{1,0:T(8,128)(2,1)S(1)}, bf16[1024,768]{1,0:T(8,128)(2,1)}, u32[]{:S(2)}) copy-start(bf16[1024,768]{1,0:T(8,128)(2,1)} %param.23) | copy-start | bytes 4718596
  277.7 7.7 %copy-start.9 = (f32[1024,1536]{1,0:T(8,128)S(1)}, f32[1024,1536]{1,0:T(8,128)}, u32[]{:S(2)}) copy-start(f32[1024,1536]{1,0:T(8,128)} %get-tuple-element.51) | copy-start | bytes 18874372
  277.7 17.1 %slice-start = ((s8[6291456]{0:T(1024)(128)(4,1)}), s8[4194304]{0:T(1024)(128)(4,1)S(1)}, s32[]{:S(2)}) async-start(s8[6291456]{0:T(1024)(128)(4,1)} %bitcast.318), calls=%async_computation.8 | async-start | bytes 8388608
  285.4 9.4 %slice-start.1 = ((s8[6291456]{0:T(1024)(128)(4,1)}), s8[2097152]{0:T(1024)(128)(4,1)S(1)}, s32[]{:S(2)}) async-start(s8[6291456]{0:T(1024)(128)(4,1)} %bitcast.318), calls=%async_computation.9 | async-start | bytes 4194304
  294.8 3.1 copy-start.7
  298.7 222.3 %reduce-scatter.5.cloned.1.call-start = ((), (), s32[]{:S(2)}) async-start(), calls=%async_computation.6 | async-start | bytes 2433024 | tf_op jit(solution)/shard_map/reduce_scatter | solution.py:344
  306.6 312.1 %reduce-scatter.7.cloned.1.call-start = ((), (), s32[]{:S(2)}) async-start(), calls=%async_computation.7 | async-start | bytes 5474304
  482.3 3.0 copy-start.5
  482.3 5.1 copy-start.6
  487.9 13.8 %collective-permute-start.1 = (f32[3,1792]{1,0:T(4,128)S(1)}, f32[3,1792]{1,0:T(4,128)S(1)}, u32[]{:S(2)}, u32[]{:S(2)}) collective-permute-start(f32[3,1792]{1,0:T(4,128)S(1)} %pad_add_fusion.1), channel_id=1, source_target_pairs={{1,0},{2,1},{3,2},{4,3},{5,4},{6,5},{7,6},{9,8},{10,9},{11,10},{12... | collective-permute-start | bytes 64520 | tf_op jit(solution)/shard_map/ppermute | solution.py:24
  500.0 4.2 copy-start.10
  500.0 4.2 copy-start.12
  528.3 57.3 %copy-start.15 = (f32[1024]{0:T(1024)S(1)}, f32[1024]{0:T(1024)}, u32[]{:S(2)}) copy-start(f32[1024]{0:T(1024)} %copy-done.14) | copy-start | bytes 12292
  540.0 87.9 %copy-start.1 = (bf16[96,3352]{1,0:T(8,128)(2,1)S(1)}, bf16[96,3352]{1,0:T(8,128)(2,1)}, u32[]{:S(2)}) copy-start(bf16[96,3352]{1,0:T(8,128)(2,1)} %param.15) | copy-start | bytes 1930756
  (4 other events, 5.6 us)
Sparse Core Ops, SparseCore 0:
  11.4 68.4 all-gather.6
  157.7 60.5 all-gather.8
  221.8 55.9 all-gather.10
  298.8 59.6 all-gather.12
  363.6 97.7 reduce-scatter.4
  513.9 104.7 reduce-scatter.6

commit v2 on v1

--- a/solution.py
+++ b/solution.py
@@ -16,6 +16,7 @@
 
 EPSILON = 1e-05
 WRAP_IDS = 256
+MAX_LEN = 4096
 
 
 def passed_along(shard, axis, by):
@@ -77,10 +78,10 @@
 TN = ((0,), (0,))
 
 
-def block_mask(segc_ref, segr_ref):
+def block_mask(segc_ref, segr_ref, reader):
     span = segc_ref.shape[0]
-    at = lax.broadcasted_iota(jnp.int32, (span, span), 0)
-    of = lax.broadcasted_iota(jnp.int32, (span, span), 1)
+    at = lax.broadcasted_iota(jnp.int32, (span, span), reader)
+    of = lax.broadcasted_iota(jnp.int32, (span, span), 1 - reader)
     keep = (segc_ref[:, 0:1] == segr_ref[0:1, :]) & (at >= of)
     return jnp.where(keep, 0.0, MASKED)
 
@@ -104,7 +105,7 @@
 
     b_mat = conv_ref[:, DI : DI + N]
     c_mat = conv_ref[:, DI + N :]
-    bias[...] = block_mask(segc_ref, segr_ref)
+    bias[...] = block_mask(segc_ref, segr_ref, 0)
     scores[...] = mm(c_mat, b_mat, NT)
     enter_ref[0] = state[...]
     lane = lax.broadcasted_iota(jnp.int32, (span, wide), 1)
@@ -149,8 +150,8 @@
 
     b_mat = conv_ref[:, DI : DI + N]
     c_mat = conv_ref[:, DI + N :]
-    bias[...] = block_mask(segc_ref, segr_ref)
-    scores[...] = mm(c_mat, b_mat, NT)
+    bias[...] = block_mask(segc_ref, segr_ref, 1)
+    scores[...] = mm(b_mat, c_mat, NT)
     gscores[...] = jnp.zeros_like(gscores)
     gbc[...] = jnp.zeros_like(gbc)
     lane = lax.broadcasted_iota(jnp.int32, (span, wide), 1)
@@ -170,18 +171,18 @@
         gy = gmix_ref[:, at]
         gyb = gy.astype(jnp.bfloat16)
         parts = []
-        row_sums = []
+        col_sums = []
         for a in range(2):
-            gaps = cols[:, a : a + 1] - rows_ref[j, a : a + 1, :]
+            gaps = rows_ref[j, a : a + 1, :] - cols[:, a : a + 1]
             e = jnp.exp(gaps + bias[...])
             w = e * scores[...]
             mine = low if a == 0 else jnp.logical_not(low)
-            dw = mm(jnp.where(mine, gy, 0.0), xb, NT)
+            dw = mm(xb, jnp.where(mine, gy, 0.0), NT)
             gscores[...] += e * dw
             q = w * dw
-            row_sums.append(jnp.sum(q, axis=1, keepdims=True))
+            col_sums.append(jnp.sum(q, axis=1, keepdims=True))
             grows_ref[j, a : a + 1, :] = jnp.sum(q, axis=0, keepdims=True)
-            parts.append(mm(w, gyb, TN))
+            parts.append(mm(w, gyb, NN))
         gx = jnp.where(low, parts[0], parts[1])
         enter = pair_columns(cols, 4)
         leave = pair_columns(cols, 6)
@@ -209,7 +210,7 @@
             tail = tail + jnp.sum(
                 kept[a * P_SIZE : (a + 1) * P_SIZE], axis=0, keepdims=True
             )
-            gcum = row_sums[a] + jnp.sum(jnp.where(mine, v1, 0.0), axis=1, keepdims=True)
+            gcum = jnp.sum(jnp.where(mine, v1, 0.0), axis=1, keepdims=True) - col_sums[a]
             gcum = gcum + jnp.where(last, tail, 0.0)
             gdt = jnp.sum(jnp.where(mine, v2, 0.0), axis=1, keepdims=True)
             out = jnp.where(lane8 == a, gcum, out)
@@ -220,8 +221,8 @@
         gstate[at, :] = through + mm(gye, c_mat, TN)
 
     gs = gscores[...].astype(jnp.bfloat16)
-    gconv_ref[:, DI : DI + N] = gbc[:, :N] + mm(gs, c_mat, TN)
-    gconv_ref[:, DI + N :] = gbc[:, N:] + mm(gs, b_mat, NN)
+    gconv_ref[:, DI : DI + N] = gbc[:, :N] + mm(gs, c_mat, NN)
+    gconv_ref[:, DI + N :] = gbc[:, N:] + mm(gs, b_mat, TN)
 
 
 def scan_specs(count, order):
@@ -293,25 +294,23 @@
     )(conv_b, g_mixed, cols, rows, segc, segr, skip, states, g_out)
 
 
-def carried(state, gain, reverse):
-    count, mine = (lax.axis_size("shard"), lax.axis_index("shard"))
-    sent = jnp.concatenate(
-        [state, jnp.pad(gain[None, :], ((0, 15), (0, N - H)))], axis=0
-    ).astype(jnp.bfloat16)
-    everything = lax.all_gather(sent, "shard")
-    gains = everything[:, DI, :H].astype(jnp.float32)
-    weights = [None] * count
-    run = jnp.ones((H,), jnp.float32)
-    for k in range(count) if reverse else reversed(range(count)):
-        counts = k > mine if reverse else k < mine
-        weights[k] = jnp.where(counts, run, 0.0)
-        run = jnp.where(counts, run * gains[k], run)
-    total = jnp.zeros((H, P_SIZE, N), jnp.float32)
-    for k in range(count):
-        total = total + weights[k][:, None, None] * everything[k, :DI].reshape(
-            H, P_SIZE, N
-        ).astype(jnp.float32)
-    return total.reshape(DI, N)
+def carried(state, gain, reverse, tokens_here):
+    reach = min(lax.axis_size("shard") - 1, -(-MAX_LEN // tokens_here))
+    sign = -1 if reverse else 1
+
+    def arriving(state, gain, by):
+        tail = jnp.pad(gain[None, :], ((0, 15), (0, N - H)))
+        sent = jnp.concatenate([state, tail], axis=0).astype(jnp.bfloat16)
+        got = passed_along(sent, "shard", sign * by).astype(jnp.float32)
+        return got[:DI], got[DI, :H]
+
+    covered = 1
+    while covered < reach:
+        far_state, far_gain = arriving(state, gain, covered)
+        state = far_state * jnp.repeat(gain, P_SIZE)[:, None] + state
+        gain = far_gain * gain
+        covered *= 2
+    return arriving(state, gain, 1)[0]
 
 
 def gather_params(w_in, w_out, conv_w, conv_b, norm_gain, gate_gain):
@@ -331,7 +330,8 @@
     c = b + norm_gain.size
     full_conv = small[:, :a].reshape(count, KC, -1).transpose(1, 0, 2).reshape(KC, -1)
     return (
-        whole(w_in),
+        whole(w_in[:, DI:]),
+        whole(w_in[:, :DI]),
         whole(w_out),
         full_conv.astype(jnp.float32),
         small[:, a:b].reshape(-1).astype(jnp.float32),
@@ -361,7 +361,7 @@
     w_out,
     cotangent,
 ):
-    full_in, full_out, full_conv, full_bias, full_norm, full_gate = gather_params(
+    in_rest, in_z, full_out, full_conv, full_bias, full_norm, full_gate = gather_params(
         w_in, w_out, conv_w, conv_b, norm_gain, gate_gain
     )
     rim_len = KC - 1
@@ -375,8 +375,8 @@
 
     normed, norm_pull = jax.vjp(norm_piece, tok_f, full_norm)
     normed_b = normed.astype(jnp.bfloat16)
-    projected = jnp.dot(normed_b, full_in, preferred_element_type=jnp.float32).astype(jnp.bfloat16)
-    xbc_b = projected[:, DI : DI + CONV]
+    projected = mm(normed_b, in_rest, NN).astype(jnp.bfloat16)
+    xbc_b = projected[:, :CONV]
     rim = jnp.concatenate(
         [
             xbc_b[-rim_len:],
@@ -390,8 +390,7 @@
     prev_last = jnp.where(lax.axis_index("shard") == 0, 0, prev_segs[-1])
     xbc_f = xbc_b.astype(jnp.float32)
     rim_f = rim_rows.astype(jnp.float32)
-    gate_z = projected[:, :DI].astype(jnp.float32)
-    dt_raw = projected[:, DI + CONV :].astype(jnp.float32)
+    dt_raw = projected[:, CONV:].astype(jnp.float32)
 
     def conv_piece(xbc_in, rim_in, weight_in, bias_in):
         return causal_conv(xbc_in, rim_in, weight_in, bias_in, wrapped, prev_segs)
@@ -437,7 +436,10 @@
     skip = jnp.repeat(d_skip, P_SIZE)[None, :]
 
     local_mixed, local_states, local_state = scan_forward(conv_bf, cols, rows, segc, segr, skip)
-    state_in = carried(local_state, carry_gain, False)
+    local_state, in_z = lax.optimization_barrier((local_state, in_z))
+    gate_z = mm(normed_b, in_z, NN).astype(jnp.bfloat16).astype(jnp.float32)
+    state_in = carried(local_state, carry_gain, False, count)
+    state_in, full_out = lax.optimization_barrier((state_in, full_out))
     c_mat = conv_bf[:, DI + N :]
     running_wide = jnp.repeat(running, P_SIZE, axis=1)
     mixed_out = local_mixed + mm(c_mat, state_in, NT) * running_wide
@@ -450,8 +452,10 @@
     grad_out_full = mm(gated_b, cotangent, TN)
     part_out = owned_sum(grad_out_full)
     g_mixed, g_gate_z, g_gate_gain = gate_pull(g_gated)
+    g_z_b = g_gate_z.astype(jnp.bfloat16)
+    part_z = owned_sum(mm(normed_b, g_z_b, TN))
     seed_grad = mm(g_mixed * running_wide, c_mat, TN)
-    state_out_grad = carried(seed_grad, carry_gain, True)
+    state_out_grad = carried(seed_grad, carry_gain, True, count)
     states = (
         local_states
         + jnp.repeat(entering_gain, P_SIZE, axis=1)[:, :, None] * state_in[None]
@@ -462,7 +466,7 @@
     g_d_skip = g_skip.reshape(H, P_SIZE).sum(1)
     g_cols = g_cols[:, :, :4].reshape(pairs, count, 2, 2).transpose(2, 1, 0, 3)
     g_cols = g_cols.reshape(2, count, H)
-    g_cum = g_cols[0] - g_rows.reshape(H, count).T
+    g_cum = g_cols[0] + g_rows.reshape(H, count).T
     g_decay = jnp.einsum(
         "ts,bth->bsh", lower, g_cum.reshape(blocks, SPAN, H), precision=HIGH
     ).reshape(count, H)
@@ -474,10 +478,10 @@
     g_xbc, g_rim, g_conv_w, g_conv_b = conv_pull(g_conv)
     from_next = passed_along(g_rim, "shard", -1)
     g_xbc = g_xbc + jnp.pad(from_next, ((count - rim_len, 0), (0, 0)))
-    g_projected = jnp.concatenate([g_gate_z, g_xbc, g_dt_raw], axis=1).astype(jnp.bfloat16)
+    g_projected = jnp.concatenate([g_xbc, g_dt_raw], axis=1).astype(jnp.bfloat16)
     grad_in_full = mm(normed_b, g_projected, TN)
-    part_in = owned_sum(grad_in_full)
-    g_normed = mm(g_projected, full_in, NT)
+    part_in = jnp.concatenate([part_z, owned_sum(grad_in_full)], axis=1)
+    g_normed = mm(g_projected, in_rest, NT) + mm(g_z_b, in_z, NT)
     g_tokens, g_norm_gain = norm_pull(g_normed)
     grad_tokens = cotangent.astype(jnp.float32) + g_tokens
 

time: 643 us -> 536 us (0.83)
  waiting for transfers between devices: 198 us -> 79.2 us
  starting transfers between devices: 5.49 us -> 20.9 us
  other arithmetic: 100 us -> 89 us
  blocking collectives: 89.1 us -> 99.4 us
    all_gather x2 -> x0, waiting for transfers between devices: 94.1 us -> none  [carried(): everything = lax.all_gather(sent, 'shard')]
    all_gather x2 -> x3, waiting for transfers between devices: 75.3 us -> 25.5 us  [whole(): return lax.all_gather(part, ('shard', 'replica'), axis=0, tiled=True)]
    ppermute x2 -> x8, waiting for transfers between devices: 0.01 us -> 34.8 us  [passed_along(): return lax.ppermute(shard, axis, pairs)]
    ppermute x2 -> x8, starting transfers between devices: 4.86 us -> 20.4 us  [passed_along(): return lax.ppermute(shard, axis, pairs)]
    dot_general x6 -> x10, matrix products: 51.4 us -> 66 us  [mm(): lax.dot_general(a.astype(jnp.bfloat16), b.astype(jnp.bfloat16), (dims, ((...]
    unnamed x7, waiting for transfers between devices: 28.2 us -> 18.8 us
    dot_general x1 -> x0, matrix products: 9.08 us -> none  [body(): jnp.dot(normed_b, full_in, preferred_element_type=jnp.float32)]
    another operation x3 -> x9, other arithmetic: 10.8 us -> 3.64 us
  transfers between devices with their start and end apart: 8 -> 14, of which waited for: 5 -> 8; matrix products, arithmetic and copies ran while one was open for 22% -> 35% of each run, Pallas kernels for 13% -> 20%
where the time goes in v2:
time: 536 us; the launch traced here: 527 us
  Pallas kernels  107 us (20%)
  blocking collectives  99.4 us (19%)
  other arithmetic  89 us (17%)
  waiting for transfers between devices  79.2 us (15%)
  matrix products  72.6 us (14%)
  local copies, waits for them, and re-layouts  42.9 us (8%)
  starting transfers between devices  20.9 us (4%)
  between operations  16 us (3%)
    pallas_call x1, Pallas kernels, scan_backward(): pl.pallas_call(backward_kernel, grid=(count,), in_specs=[s['conv'], s['mi...  77.3 us
    dot_general x10, matrix products, mm(): lax.dot_general(a.astype(jnp.bfloat16), b.astype(jnp.bfloat16), (dims, ((...  66 us
    psum x1, blocking collectives, body(): flat = lax.psum(flat, ('replica', 'shard')).reshape(-1)  46.1 us
    ppermute x8, waiting for transfers between devices, passed_along(): return lax.ppermute(shard, axis, pairs)  34.8 us
    all_gather x1, blocking collectives, gather_params(): small = lax.all_gather(small, 'shard', axis=0)  32.5 us
    pallas_call x1, Pallas kernels, scan_forward(): pl.pallas_call(forward_kernel, grid=(count,), in_specs=[s['conv'], s['col...  30.1 us
    all_gather x3, waiting for transfers between devices, whole(): return lax.all_gather(part, ('shard', 'replica'), axis=0, tiled=True)  25.5 us
    all_gather x3, blocking collectives, owned_sum(): lax.all_gather(part, 'replica', axis=0, tiled=True).astype(jnp.float32)  20.9 us
  transfers between devices with their start and end apart: 14, of which 8 were waited for; matrix products, arithmetic and copies ran while one was open for 35% of the time, Pallas kernels for 20%

profile of v2, /device:TPU:0, one launch (start us, length us, event | category | flops | bytes accessed | tf_op | source)
XLA Modules:
  0.0 527.4 jit_solution(4182367141673475452)
XLA Ops:
  15.4 32.5 %all-gather.1 = bf16[8,1,1408]{2,1,0:T(2,128)(2,1)S(1)} all-gather(bf16[1,1,1408]{2,1,0:T(2,128)(2,1)S(1)} %reshape.315), channel_id=2, replica_groups=mesh['replica'=4,'shard'=8] {'shard'}, dimensions={0}, use_global_device_ids=true | all-gather | bytes 25344 | tf_op jit(solution)/shard_map/all_gather | solution.py:326
  53.3 19.7 %all-gather.6.cloned.1.call-done = bf16[768,1816]{1,0:T(8,128)(2,1)} async-done(((bf16[24,1816]{1,0:T(8,128)(2,1)}), bf16[768,1816]{1,0:T(8,128)(2,1)}) %all-gather.6.cloned.1.call-update) | async-done | bytes 2789392 | tf_op jit(solution)/shard_map/all_gather | solution.py:323
  91.0 19.8 %multiply_convert_fusion = (bf16[1024,1792]{1,0:T(8,128)(2,1)}, f32[1024,1792]{1,0:T(8,128)}) fusion(f32[1024,1792]{1,0:T(8,128)} %slice_convert_fusion, f32[1792]{0:T(1024)S(1)} %mul.443, f32[1024]{0:T(1024)S(1)} %get-tuple-element.76, f32[3,1792]{1,0:T(4,128)S(1)} %slice_convert_fusion.3, f32[1792]{0:T(1024)S(1)} %mul.438, f32[1024]{0:T(1024)S(1)} %get-tuple-element.77, ...), kind=kLoop, calls=%fused_computation.20 | loop fusion | flops 34865152 | bytes 18419712 | tf_op jit(solution)/shard_map/convert_element_type | solution.py:399
  115.0 30.1 %shard_map.203 = (f32[1024,1536]{1,0:T(8,128)}, f32[4,1536,128]{2,1,0:T(8,128)S(1)}, f32[1536,128]{1,0:T(8,128)S(1)}) custom-call(bf16[1024,1792]{1,0:T(8,128)(2,1)} %get-tuple-element.52.conv_ref, f32[12,1024,8]{2,1,0:T(8,128)} %copy.105.cols_ref, f32[12,2,1024]{2,1,0:T(2,128)S(1)} %bitcast.111, s32[1024,1]{1,0:T(8,128)S(1)} %copy.106.segc_ref, ...), custom_call_target="tpu_custom_call" | custom-call | tf_op jit(solution)/shard_map/pallas_call | solution.py:248
  150.1 8.1 %collective-permute-done.1 = bf16[1552,128]{1,0:T(8,128)(2,1)S(1)} collective-permute-done((bf16[1552,128]{1,0:T(8,128)(2,1)S(1)}, bf16[1552,128]{1,0:T(8,128)(2,1)S(1)}, u32[]{:S(2)}, u32[]{:S(2)}) %collective-permute-start.1) | collective-permute-done | bytes 397344 | tf_op jit(solution)/shard_map/ppermute | solution.py:25
  158.8 6.5 %collective-permute-start.2 = (bf16[1552,128]{1,0:T(8,128)(2,1)S(1)}, bf16[1552,128]{1,0:T(8,128)(2,1)}, u32[]{:S(2)}, u32[]{:S(2)}) collective-permute-start(bf16[1552,128]{1,0:T(8,128)(2,1)S(1)} %fusion.38), channel_id=1, source_target_pairs={{0,2},{1,3},{2,4},{3,5},{4,6},{5,7},{8,10},{9,11},{10,12},{11,13},... | collective-permute-start | bytes 1191944 | tf_op jit(solution)/shard_map/ppermute | solution.py:25
  169.4 6.5 %copy.109 = f32[1024,1536]{1,0:T(8,128)} copy(f32[1024,1536]{0,1:T(8,128)} %bitcast.118) | data formatting | bytes 12582912 | tf_op jit(solution)/shard_map/reshape | solution.py:444
  179.0 6.5 %convolution_convert_fusion = bf16[1024,1536]{1,0:T(8,128)(2,1)} fusion(bf16[768,1536]{1,0:T(8,128)(2,1)} %all-gather.8.cloned.1.call-done, bf16[1024,768]{1,0:T(8,128)(2,1)} %param.12, f32[768]{0:T(1024)S(1)} %reshape.311, f32[1024]{0:T(1024)S(1)} %fusion.67), kind=kOutput, calls=%fused_computation.47 | convolution fusion | flops 2420637696 | bytes 7085056 | tf_op jit(solution)/shard_map/dot_general | solution.py:68
  195.7 7.2 %multiply_reduce_fusion.5 = (f32[1024]{0:T(1024)S(1)}, f32[1024,1536]{1,0:T(8,128)S(1)}) fusion(bf16[1024,1536]{1,0:T(8,128)(2,1)} %convolution_convert_fusion, f32[1024,1536]{1,0:T(8,128)} %get-tuple-element.22, f32[1024,1536]{1,0:T(8,128)} %copy.109, f32[1536,128]{1,0:T(8,128)S(1)} %slice_convert_fusion.2, bf16[1024,1792]{1,0:T(8,128)(2,1)} %get-tuple-element.52.conv_ref), kind=kOutput, calls=%fused_computation.38 | convolution fusion | flops 418577408 | bytes 23072768 | tf_op jit(solution)/shard_map/dot_general | solution.py:68
  211.3 7.7 %fusion.11 = (f32[1536]{0:T(1024)S(1)}, f32[1024]{0:T(1024)S(1)}, f32[1536,1024]{0,1:T(8,128)S(1)}) fusion(f32[1024]{0:T(1024)S(1)} %fusion.68, f32[1024,1536]{1,0:T(8,128)} %copy-done.8, bf16[1024,1536]{1,0:T(8,128)(2,1)} %convolution_convert_fusion, f32[1536]{0:T(1024)S(1)} %reshape.312, bf16[1536,768]{1,0:T(8,128)(2,1)} %all-gather.10.cloned.1.call-done, ...), kind=kOutput, calls=%fused_computation.34 | convolution fusion | flops 2434790912 | bytes 19681280 | tf_op jit(solution)/shard_map/dot_general | solution.py:68
  224.0 7.9 %fusion.93 = (bf16[1536,128]{1,0:T(8,128)(2,1)S(1)}, f32[1536,128]{1,0:T(8,128)S(1)}) fusion(bf16[1024,1792]{1,0:T(8,128)(2,1)} %get-tuple-element.52.conv_ref, f32[1024,1536]{1,0:T(8,128)S(1)} %get-tuple-element.56.gmix_ref, f32[1024,1536]{1,0:T(8,128)} %copy.109), kind=kOutput, calls=%fused_computation.209 | convolution fusion | flops 405995520 | bytes 14024704 | tf_op jit(solution)/shard_map/dot_general | solution.py:68
  238.7 6.5 %collective-permute-done.4 = bf16[1552,128]{1,0:T(8,128)(2,1)S(1)} collective-permute-done((bf16[1552,128]{1,0:T(8,128)(2,1)S(1)}, bf16[1552,128]{1,0:T(8,128)(2,1)S(1)}, u32[]{:S(2)}, u32[]{:S(2)}) %collective-permute-start.4) | collective-permute-done | bytes 397344 | tf_op jit(solution)/shard_map/ppermute | solution.py:25
  253.3 6.7 %collective-permute-done.5 = bf16[1552,128]{1,0:T(8,128)(2,1)} collective-permute-done((bf16[1552,128]{1,0:T(8,128)(2,1)}, bf16[1552,128]{1,0:T(8,128)(2,1)}, u32[]{:S(2)}, u32[]{:S(2)}) %collective-permute-start.5) | collective-permute-done | bytes 397344 | tf_op jit(solution)/shard_map/ppermute | solution.py:25
  265.0 9.2 %collective-permute-done.6 = bf16[1552,128]{1,0:T(8,128)(2,1)S(1)} collective-permute-done((bf16[1552,128]{1,0:T(8,128)(2,1)S(1)}, bf16[1552,128]{1,0:T(8,128)(2,1)S(1)}, u32[]{:S(2)}, u32[]{:S(2)}) %collective-permute-start.6) | collective-permute-done | bytes 397344 | tf_op jit(solution)/shard_map/ppermute | solution.py:25
  274.2 77.3 %shard_map.204 = (f32[1024,1792]{1,0:T(8,128)}, f32[12,1024,8]{2,1,0:T(8,128)}, f32[12,2,1024]{2,1,0:T(2,128)S(1)}, f32[1,1536]{1,0:T(1,128)S(1)}) custom-call(bf16[1024,1792]{1,0:T(8,128)(2,1)} %get-tuple-element.52.conv_ref, f32[1024,1536]{1,0:T(8,128)} %copy-done.4, f32[12,1024,8]{2,1,0:T(8,128)} %copy.105.cols_ref, f32[12,2,1024]{2,1,0:T(2,128)S(1)} %bitcast.112, ...), custom_call_target="tpu_custom_call" | custom-call | tf_op jit(solution)/shard_map/pallas_call | solution.py:272
  356.4 17.6 %multiply_reduce_fusion.2 = (f32[1792]{0:T(1024)S(1)}, f32[1792]{0:T(1024)S(1)}, f32[1792]{0:T(1024)S(1)}, f32[1792]{0:T(1024)S(1)}, f32[1792]{0:T(1024)S(1)}, /*index=5*/f32[1024,1792]{1,0:T(8,128)S(1)}) fusion(f32[1024,1792]{1,0:T(8,128)} %slice_convert_fusion, f32[3,1792]{1,0:T(4,128)S(1)} %slice_convert_fusion.3, f32[1024]{0:T(1024)S(1)} %get-tuple-element.76, ...), kind=kLoop, calls=%fused_computation.18 | loop fusion | flops 45866240 | bytes 33099776 | tf_op jit(solution)/shard_map/transpose(jvp())/reduce_sum | solution.py:44
  374.0 11.0 %broadcast_multiply_fusion = (f32[1024,1792]{1,0:T(8,128)}, f32[1024,1792]{1,0:T(8,128)}, f32[1024,1792]{1,0:T(8,128)}, f32[1024,1792]{1,0:T(8,128)}) fusion(f32[1024,1792]{1,0:T(8,128)S(1)} %get-tuple-element.51, f32[1792]{0:T(1024)S(1)} %mul.443, f32[1024]{0:T(1024)S(1)} %get-tuple-element.75, f32[1792]{0:T(1024)S(1)} %mul.422, ...), kind=kLoop, calls=%fused_computation.52 | loop fusion | flops 12845056 | bytes 36741120 | tf_op jit(solution)/shard_map/transpose(jvp())/mul | solution.py:44
  390.0 8.7 %pad_add_fusion = f32[1027,1792]{1,0:T(8,128)S(1)} fusion(f32[1024,1792]{1,0:T(8,128)} %get-tuple-element.59, f32[1024,1792]{1,0:T(8,128)} %get-tuple-element.60, f32[1024,1792]{1,0:T(8,128)} %get-tuple-element.61, f32[1024,1792]{1,0:T(8,128)S(1)} %bitcast.117), kind=kLoop, calls=%fused_computation.8 | loop fusion | flops 5521152 | bytes 36721664 | tf_op jit(solution)/shard_map/transpose(jvp())/add_any | solution.py:44
  408.1 7.0 %fusion.94 = f32[1024,768]{1,0:T(8,128)} fusion(bf16[1024,1536]{1,0:T(8,128)(2,1)} %copy-done.11, bf16[768,1536]{1,0:T(8,128)(2,1)} %all-gather.8.cloned.1.call-done), kind=kOutput, calls=%fused_computation.210 | convolution fusion | flops 2415919104 | bytes 8650752 | tf_op jit(solution)/shard_map/dot_general | solution.py:68
  415.4 9.5 %fusion.15 = (f32[768]{0:T(1024)S(1)}, f32[1024]{0:T(1024)S(1)}, f32[1024,768]{1,0:T(8,128)}) fusion(bf16[1024,768]{1,0:T(8,128)(2,1)S(1)} %copy-done.7, f32[1024]{0:T(1024)S(1)} %fusion.67, f32[768]{0:T(1024)S(1)} %reshape.311, f32[1024,768]{1,0:T(8,128)} %fusion.94, bf16[768,1816]{1,0:T(8,128)(2,1)} %all-gather.6.cloned.1.call-done, ...), kind=kOutput, calls=%fused_computation.57 | convolution fusion | flops 2870049024 | bytes 14387200 | tf_op jit(solution)/shard_map/dot_general | solution.py:68
  425.0 46.1 %psum.7 = f32[96,128]{1,0:T(8,128)S(1)} all-reduce(f32[96,128]{1,0:T(8,128)S(1)} %pad_bitcast_fusion), channel_id=1, replica_groups=mesh['replica'=4,'shard'=8] {'replica','shard'}, use_global_device_ids=true, to_apply=%region_14.15 | all-reduce | flops 12288 | bytes 98304 | tf_op jit(solution)/shard_map/psum | solution.py:493
  478.8 8.1 %all_gather.31 = bf16[192,768]{1,0:T(8,128)(2,1)S(1)} all-gather(bf16[48,768]{1,0:T(8,128)(2,1)} %reduce-scatter.8.cloned.1.call-done), channel_id=1, replica_groups=mesh['replica'=4,'shard'=8] {'replica'}, dimensions={0}, use_global_device_ids=true | all-gather | bytes 368640 | tf_op jit(solution)/shard_map/all_gather | solution.py:347
  494.0 18.7 %reduce-scatter.10.cloned.1.call-done = bf16[24,1816]{1,0:T(8,128)(2,1)} async-done(((bf16[768,1816]{1,0:T(8,128)(2,1)}), bf16[24,1816]{1,0:T(8,128)(2,1)}) %reduce-scatter.10.cloned.1.call-update) | async-done | bytes 87184
  512.7 6.5 %all_gather.30 = bf16[96,1816]{1,0:T(8,128)(2,1)S(1)} all-gather(bf16[24,1816]{1,0:T(8,128)(2,1)} %reduce-scatter.10.cloned.1.call-done), channel_id=1, replica_groups=mesh['replica'=4,'shard'=8] {'replica'}, dimensions={0}, use_global_device_ids=true | all-gather | bytes 435840 | tf_op jit(solution)/shard_map/all_gather | solution.py:347
  (245 shorter events, 126.2 us)
Async XLA Ops:
  7.2 65.8 %all-gather.6.cloned.1.call-start = ((), (), s32[]{:S(2)}) async-start(), calls=%async_computation.3 | async-start | bytes 3041280 | tf_op jit(solution)/shard_map/all_gather | solution.py:323
  9.0 137.7 %all-gather.8.cloned.1.call-start = ((), (), s32[]{:S(2)}) async-start(), calls=%async_computation.4 | async-start | bytes 2433024 | tf_op jit(solution)/shard_map/all_gather | solution.py:323
  10.7 185.0 %all-gather.10.cloned.1.call-start = ((), (), s32[]{:S(2)}) async-start(), calls=%async_computation.5 | async-start | bytes 2433024 | tf_op jit(solution)/shard_map/all_gather | solution.py:323
  11.4 467.3 %reduce-scatter.8.cloned.1.call-start = ((), (), s32[]{:S(2)}) async-start(), calls=%async_computation.7 | async-start | bytes 2433024 | tf_op jit(solution)/shard_map/reduce_scatter | solution.py:344
  49.2 36.9 %copy-start.25 = (f32[24]{0:T(128)}, f32[24]{0:T(128)S(1)}, u32[]{:S(2)}) copy-start(f32[24]{0:T(128)S(1)} %get-tuple-element.83) | copy-start | bytes 292
  78.8 10.7 %copy-start.22 = (s32[1024]{0:T(1024)S(1)}, s32[1024]{0:T(1024)}, u32[]{:S(2)}) copy-start(s32[1024]{0:T(1024)} %param.13) | copy-start | bytes 12292
  82.7 5.6 %collective-permute-start = (bf16[3,1920]{1,0:T(4,128)(2,1)S(1)}, bf16[3,1920]{1,0:T(4,128)(2,1)S(1)}, u32[]{:S(2)}, u32[]{:S(2)}) collective-permute-start(bf16[3,1920]{1,0:T(4,128)(2,1)S(1)} %pad_maximum_fusion.8), channel_id=1, source_target_pairs={{0,1},{1,2},{2,3},{3,4},{4,5},{5,6},{6,7},{8,9},{9,10},{10,11},{11... | collective-permute-start | bytes 34568 | tf_op jit(solution)/shard_map/ppermute | solution.py:25
  111.0 66.2 %copy-start.14 = (f32[1024,24]{1,0:T(8,128)}, f32[1024,24]{1,0:T(8,128)S(1)}, u32[]{:S(2)}) copy-start(f32[1024,24]{1,0:T(8,128)S(1)} %bitcast_multiply_fusion.4) | copy-start | bytes 294916
  146.8 11.5 %collective-permute-start.1 = (bf16[1552,128]{1,0:T(8,128)(2,1)S(1)}, bf16[1552,128]{1,0:T(8,128)(2,1)S(1)}, u32[]{:S(2)}, u32[]{:S(2)}) collective-permute-start(bf16[1552,128]{1,0:T(8,128)(2,1)S(1)} %pad_maximum_fusion.7), channel_id=1, source_target_pairs={{0,1},{1,2},{2,3},{3,4},{4,5},{5,6},{6,7},{8,9},{9,10},{10,11},{11... | collective-permute-start | bytes 1191944 | tf_op jit(solution)/shard_map/ppermute | solution.py:25
  158.8 17.3 %collective-permute-start.2 = (bf16[1552,128]{1,0:T(8,128)(2,1)S(1)}, bf16[1552,128]{1,0:T(8,128)(2,1)}, u32[]{:S(2)}, u32[]{:S(2)}) collective-permute-start(bf16[1552,128]{1,0:T(8,128)(2,1)S(1)} %fusion.38), channel_id=1, source_target_pairs={{0,2},{1,3},{2,4},{3,5},{4,6},{5,7},{8,10},{9,11},{10,12},{11,13},... | collective-permute-start | bytes 1191944 | tf_op jit(solution)/shard_map/ppermute | solution.py:25
  177.7 12.2 %collective-permute-start.3 = (bf16[1552,128]{1,0:T(8,128)(2,1)S(1)}, bf16[1552,128]{1,0:T(8,128)(2,1)S(1)}, u32[]{:S(2)}, u32[]{:S(2)}) collective-permute-start(bf16[1552,128]{1,0:T(8,128)(2,1)S(1)} %fusion.39), channel_id=1, source_target_pairs={{0,1},{1,2},{2,3},{3,4},{4,5},{5,6},{6,7},{8,9},{9,10},{10,11},{11... | collective-permute-start | bytes 1191944 | tf_op jit(solution)/shard_map/ppermute | solution.py:25
  210.9 276.8 %reduce-scatter.6.cloned.1.call-start = ((), (), s32[]{:S(2)}) async-start(), calls=%async_computation.6 | async-start | bytes 2433024 | tf_op jit(solution)/shard_map/reduce_scatter | solution.py:344
  224.0 24.3 %copy-start.11 = (bf16[1024,1536]{1,0:T(8,128)(2,1)}, bf16[1024,1536]{1,0:T(8,128)(2,1)S(1)}, u32[]{:S(2)}) copy-start(bf16[1024,1536]{1,0:T(8,128)(2,1)S(1)} %get-tuple-element.57) | copy-start | bytes 9437188
  232.0 13.3 %collective-permute-start.4 = (bf16[1552,128]{1,0:T(8,128)(2,1)S(1)}, bf16[1552,128]{1,0:T(8,128)(2,1)S(1)}, u32[]{:S(2)}, u32[]{:S(2)}) collective-permute-start(bf16[1552,128]{1,0:T(8,128)(2,1)S(1)} %pad_maximum_fusion.6), channel_id=1, source_target_pairs={{1,0},{2,1},{3,2},{4,3},{5,4},{6,5},{7,6},{9,8},{10,9},{11,10},{12... | collective-permute-start | bytes 1191944 | tf_op jit(solution)/shard_map/ppermute | solution.py:25
  247.0 13.0 %collective-permute-start.5 = (bf16[1552,128]{1,0:T(8,128)(2,1)}, bf16[1552,128]{1,0:T(8,128)(2,1)}, u32[]{:S(2)}, u32[]{:S(2)}) collective-permute-start(bf16[1552,128]{1,0:T(8,128)(2,1)} %fusion.40), channel_id=1, source_target_pairs={{2,0},{3,1},{4,2},{5,3},{6,4},{7,5},{10,8},{11,9},{12,10},{13,11},... | collective-permute-start | bytes 1191944 | tf_op jit(solution)/shard_map/ppermute | solution.py:25
  252.4 260.3 %reduce-scatter.10.cloned.1.call-start = ((), (), s32[]{:S(2)}) async-start(), calls=%async_computation.8 | async-start | bytes 3041280
  253.3 10.7 %copy-start.3 = (f32[4,1536,128]{2,1,0:T(8,128)S(1)}, f32[4,1536,128]{2,1,0:T(8,128)}, u32[]{:S(2)}) copy-start(f32[4,1536,128]{2,1,0:T(8,128)} %copy-done.2) | copy-start | bytes 9437188
  262.3 11.9 %collective-permute-start.6 = (bf16[1552,128]{1,0:T(8,128)(2,1)S(1)}, bf16[1552,128]{1,0:T(8,128)(2,1)S(1)}, u32[]{:S(2)}, u32[]{:S(2)}) collective-permute-start(bf16[1552,128]{1,0:T(8,128)(2,1)S(1)} %fusion.41), channel_id=1, source_target_pairs={{1,0},{2,1},{3,2},{4,3},{5,4},{6,5},{7,6},{9,8},{10,9},{11,10},{12... | collective-permute-start | bytes 1191944 | tf_op jit(solution)/shard_map/ppermute | solution.py:25
  388.3 10.4 %copy-start.15 = (f32[4,256,24]{2,1,0:T(8,128)S(1)}, f32[4,256,24]{2,1,0:T(8,128)}, u32[]{:S(2)}) copy-start(f32[4,256,24]{2,1,0:T(8,128)} %copy.116) | copy-start | bytes 294916
  388.3 10.4 %copy-start.16 = (f32[1024,24]{1,0:T(8,128)S(1)}, f32[1024,24]{1,0:T(8,128)}, u32[]{:S(2)}) copy-start(f32[1024,24]{1,0:T(8,128)} %copy.117) | copy-start | bytes 294916
  388.4 12.1 %collective-permute-start.7 = (f32[3,1792]{1,0:T(4,128)S(1)}, f32[3,1792]{1,0:T(4,128)S(1)}, u32[]{:S(2)}, u32[]{:S(2)}) collective-permute-start(f32[3,1792]{1,0:T(4,128)S(1)} %pad_add_fusion.1), channel_id=1, source_target_pairs={{1,0},{2,1},{3,2},{4,3},{5,4},{6,5},{7,6},{9,8},{10,9},{11,10},{12... | collective-permute-start | bytes 64520 | tf_op jit(solution)/shard_map/ppermute | solution.py:25
  415.4 58.9 %copy-start.21 = (f32[1024]{0:T(1024)S(1)}, f32[1024]{0:T(1024)}, u32[]{:S(2)}) copy-start(f32[1024]{0:T(1024)} %copy-done.20) | copy-start | bytes 12292
  415.4 58.9 %copy-start.18 = (bf16[1024,768]{1,0:T(8,128)(2,1)S(1)}, bf16[1024,768]{1,0:T(8,128)(2,1)}, u32[]{:S(2)}) copy-start(bf16[1024,768]{1,0:T(8,128)(2,1)} %param.23) | copy-start | bytes 4718596
  474.2 46.1 %copy-start.1 = (bf16[192,768]{1,0:T(8,128)(2,1)S(1)}, bf16[192,768]{1,0:T(8,128)(2,1)}, u32[]{:S(2)}) copy-start(bf16[192,768]{1,0:T(8,128)(2,1)} %param.22) | copy-start | bytes 884740
  (21 other events, 130.3 us)
Sparse Core Ops, SparseCore 0:
  11.4 61.5 all-gather.5
  76.5 56.0 all-gather.7
  136.1 59.5 all-gather.9
  211.1 98.6 reduce-scatter.7
  315.8 98.0 reduce-scatter.5
  419.2 93.5 reduce-scatter.9
